TPU v7x, 32 devices: a whole 2x2x4 slice. The times are simulated.
32 devices in a mesh: wide: 16 (over z, y, core), narrow: 2 (over x).
Axes of the slice: x: 2, y: 2, z: 4, core: 2. Of those that a mesh axis runs over, the one named last changes fastest.
Arguments:
- layer_input: bfloat16 [2048, 119, 192], P(('wide', 'narrow')), may hold values from -6 to 6
- mask: int32 [2048, 119], P(('wide', 'narrow')), may hold values 0 or 1
- dout: bfloat16 [2048, 119, 192], P(('wide', 'narrow')), may hold values from -6 to 6
- attn_w: float32 [4, 192, 192], P(None, 'wide'), may hold values from -0.57735027 to 0.57735027
- ffn_in: float32 [192, 512], P('wide'), may hold values from -0.4375 to 0.4375
- ffn_out: float32 [256, 192], P('wide'), may hold values from -0.375 to 0.375
- vec: float32 [2048], P('wide'), may hold values from -1.2 to 1.6
- m_attn: float32 [4, 192, 192], P(None, 'wide'), may hold values from -112 to 112
- v_attn: float32 [4, 192, 192], P(None, 'wide'), may hold values from 24.3712 to 97.4848
- m_in: float32 [192, 512], P('wide'), may hold values from -160 to 160
- v_in: float32 [192, 512], P('wide'), may hold values from 60.928 to 243.712
- m_out: float32 [256, 192], P('wide'), may hold values from -192 to 192
- v_out: float32 [256, 192], P('wide'), may hold values from 87.73632 to 350.94528
- m_vec: float32 [2048], P('wide'), may hold values from -224 to 224
- v_vec: float32 [2048], P('wide'), may hold values from 119.41888 to 477.6755
Outputs:
- layer_output: bfloat16 [2048, 119, 192], P(('wide', 'narrow'))
- dx: bfloat16 [2048, 119, 192], P(('wide', 'narrow'))
- new_attn_w: float32 [4, 192, 192], P(None, 'wide')
- new_m_attn: float32 [4, 192, 192], P(None, 'wide')
- new_v_attn: float32 [4, 192, 192], P(None, 'wide')
- new_ffn_in: float32 [192, 512], P('wide')
- new_m_in: float32 [192, 512], P('wide')
- new_v_in: float32 [192, 512], P('wide')
- new_ffn_out: float32 [256, 192], P('wide')
- new_m_out: float32 [256, 192], P('wide')
- new_v_out: float32 [256, 192], P('wide')
- new_vec: float32 [2048], P('wide')
- new_m_vec: float32 [2048], P('wide')
- new_v_vec: float32 [2048], P('wide')
All inputs are finite; a program needn't handle non-finite values. No bound on the sum of `mask` on one device may be relied on, other than what follows from the above.
Results may differ from a plain program's by a relative error of at most 0.012.
The roundings to bfloat16 on the way count: a program that leaves them out, or rounds other values in their place, can miss the bound.
Values may be sent and summed in bfloat16 or wider, within the bound.
A program may use at most 256 MiB of HBM per device.

v0:
```python
import jax
import jax.numpy as jnp
from jax import lax
from jax.sharding import PartitionSpec as P

H = 8
FH = 256
STEP = 10


def apply_layer_norm(value):
    center = value - jnp.mean(value, -1, keepdims=True)
    inverse_deviation = lax.rsqrt(jnp.mean(center * center, -1, keepdims=True) + 1e-05)
    return (center * inverse_deviation, inverse_deviation)


def norm_backward_pass(norm_gradient, centered_input, inverse_deviation, norm_gain):
    scaled_gradient = norm_gradient * norm_gain
    input_gradient = inverse_deviation * (
        scaled_gradient
        - jnp.mean(scaled_gradient, -1, keepdims=True)
        - centered_input * jnp.mean(scaled_gradient * centered_input, -1, keepdims=True)
    )
    return (input_gradient, jnp.sum(norm_gradient * centered_input, 0), jnp.sum(norm_gradient, 0))


def matmul(left_term, right_term):
    return jnp.dot(left_term, right_term, preferred_element_type=jnp.float32)


def adamw(weight, first_m, second_m, grad, decay):
    new_m = 0.9 * first_m + 0.1 * grad
    new_v = 0.999 * second_m + 0.001 * grad * grad
    ratio = new_m / (1.0 - 0.9**STEP) / (jnp.sqrt(new_v / (1.0 - 0.999**STEP)) + 1e-08)
    return (weight - 0.1 * (ratio + decay * weight), new_m, new_v)


def on_device(
    layer_input,
    mask,
    dout,
    attn_w,
    ffn_in,
    ffn_out,
    vec,
    m_attn,
    v_attn,
    m_in,
    v_in,
    m_out,
    v_out,
    m_vec,
    v_vec,
):
    samples, length, width = layer_input.shape
    heads = H
    head_size = width // heads
    hidden_units = FH
    rows = samples * length
    factor = float(head_size) ** (-0.5)
    master = (
        attn_w.astype(jnp.bfloat16),
        ffn_in.astype(jnp.bfloat16),
        ffn_out.astype(jnp.bfloat16),
        vec.astype(jnp.bfloat16),
    )
    full = (
        lax.all_gather(master[0], "wide", axis=1, tiled=True),
        lax.all_gather(master[1], "wide", axis=0, tiled=True),
        lax.all_gather(master[2], "wide", axis=0, tiled=True),
        lax.all_gather(master[3], "wide", axis=0, tiled=True),
    )
    weights, w_in, w_out, vector16 = full
    vector = vector16.astype(jnp.float32)
    pieces = [vector[i * width : (i + 1) * width] for i in range(8)]
    (
        first_norm_gain,
        first_norm_bias,
        bias_q,
        bias_v,
        bias_o,
        second_norm_gain,
        second_norm_bias,
        bias_c2,
    ) = pieces
    bias_c1 = vector[8 * width : 8 * width + 2 * hidden_units]
    valid = (mask != 0) | (lax.broadcasted_iota(jnp.int32, mask.shape, 1) == 0)

    def scores_of(query, keyed):
        raw = (
            jnp.einsum("slhe,smhe->shlm", query, keyed, preferred_element_type=jnp.float32) * factor
        )
        return jnp.where(valid[:, None, None, :], raw, -1e30)

    input_float = layer_input.reshape(rows, width).astype(jnp.float32)
    first_centered_input, first_inverse_deviation = apply_layer_norm(input_float)
    first_normed_rows = (first_centered_input * first_norm_gain + first_norm_bias).astype(
        jnp.bfloat16
    )
    w_qkv = jnp.concatenate([weights[0], weights[1], weights[2]], axis=1)
    bias_qkv = jnp.concatenate([bias_q, jnp.zeros((width,), jnp.float32), bias_v])
    qkv = (matmul(first_normed_rows, w_qkv) + bias_qkv).astype(jnp.bfloat16)
    query = qkv[:, :width].reshape(samples, length, heads, head_size)
    keyed = qkv[:, width : 2 * width].reshape(samples, length, heads, head_size)
    valued = qkv[:, 2 * width :].reshape(samples, length, heads, head_size)
    scores = scores_of(query, keyed)
    top = jnp.max(scores, -1, keepdims=True)
    expo = jnp.exp(scores - top)
    total = jnp.sum(expo, -1, keepdims=True)
    lse = top + jnp.log(total)
    probs = expo / total
    mixed = jnp.einsum(
        "shlm,smhe->slhe", probs.astype(jnp.bfloat16), valued, preferred_element_type=jnp.float32
    )
    mixed16 = mixed.reshape(rows, width).astype(jnp.bfloat16)
    first_branch = input_float + matmul(mixed16, weights[3]) + bias_o
    second_centered_input, second_inverse_deviation = apply_layer_norm(first_branch)
    second_normed_rows = (second_centered_input * second_norm_gain + second_norm_bias).astype(
        jnp.bfloat16
    )
    gated = matmul(second_normed_rows, w_in) + bias_c1
    part_a = gated[:, :hidden_units]
    part_b = gated[:, hidden_units:]
    sigm = jax.nn.sigmoid(part_b)
    silu = part_b * sigm
    hidden16 = (part_a * silu).astype(jnp.bfloat16)
    result = first_branch + matmul(hidden16, w_out) + bias_c2
    layer_output = result.astype(jnp.bfloat16).reshape(layer_input.shape)
    back_full = (
        lax.all_gather(master[0], "wide", axis=1, tiled=True),
        lax.all_gather(master[1], "wide", axis=0, tiled=True),
        lax.all_gather(master[2], "wide", axis=0, tiled=True),
        lax.all_gather(master[3], "wide", axis=0, tiled=True),
    )
    weights_b, w_in_b, w_out_b, _ = back_full
    w_qkv_b = jnp.concatenate([weights_b[0], weights_b[1], weights_b[2]], axis=1)
    grad16 = dout.reshape(rows, width)
    gradf = grad16.astype(jnp.float32)
    d_out = matmul(hidden16.T, grad16)
    d_c2 = jnp.sum(gradf, 0)
    dhidden = matmul(grad16, w_out_b.T)
    d_a = dhidden * silu
    d_b = dhidden * part_a * sigm * (1.0 + part_b * (1.0 - sigm))
    dgated = jnp.concatenate([d_a, d_b], axis=1).astype(jnp.bfloat16)
    d_in = matmul(second_normed_rows.T, dgated)
    d_c1 = jnp.sum(dgated.astype(jnp.float32), 0)
    second_norm_gradient = matmul(dgated, w_in_b.T)
    first_branch_gradient, second_gain_gradient, second_bias_gradient = norm_backward_pass(
        second_norm_gradient, second_centered_input, second_inverse_deviation, second_norm_gain
    )
    dfirst = gradf + first_branch_gradient
    dbranch = dfirst.astype(jnp.bfloat16)
    d_wo = matmul(mixed16.T, dbranch)
    d_bo = jnp.sum(dbranch.astype(jnp.float32), 0)
    dmixed = (
        matmul(dbranch, weights_b[3].T)
        .astype(jnp.bfloat16)
        .reshape(samples, length, heads, head_size)
    )
    probs_b = jnp.exp(scores_of(query, keyed) - lse)
    d_value = jnp.einsum(
        "shlm,slhe->smhe", probs_b.astype(jnp.bfloat16), dmixed, preferred_element_type=jnp.float32
    )
    d_probs = jnp.einsum("slhe,smhe->shlm", dmixed, valued, preferred_element_type=jnp.float32)
    d_scores = (probs_b * (d_probs - jnp.sum(probs_b * d_probs, -1, keepdims=True))).astype(
        jnp.bfloat16
    )
    d_query = (
        jnp.einsum("shlm,smhe->slhe", d_scores, keyed, preferred_element_type=jnp.float32) * factor
    )
    d_key = (
        jnp.einsum("shlm,slhe->smhe", d_scores, query, preferred_element_type=jnp.float32) * factor
    )
    dqkv = jnp.concatenate(
        [d_query.reshape(rows, width), d_key.reshape(rows, width), d_value.reshape(rows, width)],
        axis=1,
    ).astype(jnp.bfloat16)
    d_wqkv = matmul(first_normed_rows.T, dqkv)
    dqkv_f = dqkv.astype(jnp.float32)
    d_bq = jnp.sum(dqkv_f[:, :width], 0)
    d_bv = jnp.sum(dqkv_f[:, 2 * width :], 0)
    first_norm_gradient = matmul(dqkv, w_qkv_b.T)
    partial_input_gradient, first_gain_gradient, first_bias_gradient = norm_backward_pass(
        first_norm_gradient, first_centered_input, first_inverse_deviation, first_norm_gain
    )
    dx = (dfirst + partial_input_gradient).astype(jnp.bfloat16).reshape(layer_input.shape)
    grad_attn = jnp.stack(
        [d_wqkv[:, :width], d_wqkv[:, width : 2 * width], d_wqkv[:, 2 * width :], d_wo]
    )
    grad_vec = jnp.concatenate(
        [
            first_gain_gradient,
            first_bias_gradient,
            d_bq,
            d_bv,
            d_bo,
            second_gain_gradient,
            second_bias_gradient,
            d_c2,
            d_c1,
        ]
    )
    local_grads = (grad_attn, d_in, d_out, grad_vec)
    summed = lax.psum((local_grads[0], local_grads[1], local_grads[2], local_grads[3]), "narrow")
    shares = (
        lax.psum_scatter(summed[0], "wide", scatter_dimension=1, tiled=True),
        lax.psum_scatter(summed[1], "wide", scatter_dimension=0, tiled=True),
        lax.psum_scatter(summed[2], "wide", scatter_dimension=0, tiled=True),
        lax.psum_scatter(summed[3], "wide", scatter_dimension=0, tiled=True),
    )
    wa, ma, va = adamw(attn_w, m_attn, v_attn, shares[0], 0.01)
    wi, mi, vi = adamw(ffn_in, m_in, v_in, shares[1], 0.01)
    wo, mo, vo = adamw(ffn_out, m_out, v_out, shares[2], 0.01)
    wv, mv, vv = adamw(vec, m_vec, v_vec, shares[3], 0.0)
    return (layer_output, dx, wa, ma, va, wi, mi, vi, wo, mo, vo, wv, mv, vv)


def solution(mesh):
    return jax.shard_map(
        on_device,
        mesh=mesh,
        in_specs=(
            P(("wide", "narrow"), None, None),
            P(("wide", "narrow"), None),
            P(("wide", "narrow"), None, None),
            P(None, "wide", None),
            P("wide", None),
            P("wide", None),
            P("wide"),
            P(None, "wide", None),
            P(None, "wide", None),
            P("wide", None),
            P("wide", None),
            P("wide", None),
            P("wide", None),
            P("wide"),
            P("wide"),
        ),
        out_specs=(
            P(("wide", "narrow"), None, None),
            P(("wide", "narrow"), None, None),
            P(None, "wide", None),
            P(None, "wide", None),
            P(None, "wide", None),
            P("wide", None),
            P("wide", None),
            P("wide", None),
            P("wide", None),
            P("wide", None),
            P("wide", None),
            P("wide"),
            P("wide"),
            P("wide"),
        ),
        check_vma=False,
    )
```

profile of v0, /device:TPU:0, one launch (start us, length us, event | category | flops | bytes accessed | tf_op | source)
XLA Modules:
  0.0 688.5 jit_solution(8976340215226160849)
XLA Ops:
  8.7 23.0 %all-gather = bf16[16,1,128]{2,1,0:T(2,128)(2,1)S(1)} all-gather(bf16[1,1,128]{2,1,0:T(2,128)(2,1)S(1)} %convert_bitcast_fusion.3), channel_id=1, replica_groups=mesh['wide'=16,'narrow'=2] {'wide'}, dimensions={0}, use_global_device_ids=true | all-gather | bytes 4352 | tf_op jit(solution)/shard_map/all_gather | solution.py:71
  44.4 19.1 %all_gather.18 = bf16[256,192]{1,0:T(8,128)(2,1)} all-gather(bf16[16,192]{1,0:T(8,128)(2,1)S(1)} %convert_element_type.101), channel_id=1, replica_groups=mesh['wide'=16,'narrow'=2] {'wide'}, dimensions={0}, use_global_device_ids=true | all-gather | bytes 104448 | tf_op jit(solution)/shard_map/all_gather | solution.py:70
  63.5 19.5 %all-gather.1 = bf16[16,12,512]{2,1,0:T(8,128)(2,1)S(1)} all-gather(bf16[1,12,512]{2,1,0:T(8,128)(2,1)S(1)} %convert_bitcast_fusion.2), channel_id=1, replica_groups=mesh['wide'=16,'narrow'=2] {'wide'}, dimensions={0}, use_global_device_ids=true | all-gather | bytes 208896 | tf_op jit(solution)/shard_map/all_gather | solution.py:69
  83.7 18.5 %all_gather.16 = bf16[4,192,192]{2,0,1:T(4,128)(2,1)S(1)} all-gather(bf16[4,12,192]{2,0,1:T(4,128)(2,1)S(1)} %convert_element_type.92), channel_id=1, replica_groups=mesh['wide'=16,'narrow'=2] {'wide'}, dimensions={1}, use_global_device_ids=true | all-gather | bytes 313344 | tf_op jit(solution)/shard_map/all_gather | solution.py:68
  130.8 14.6 %reshape.147 = bf16[64,119,8,24]{1,0,3,2:T(8,128)(2,1)} reshape(bf16[7616,192]{0,1:T(8,128)(2,1)} %get-tuple-element.87) | data formatting | bytes 5849088 | tf_op jit(solution)/shard_map/reshape | solution.py:105
  145.4 13.8 %reshape.149 = bf16[64,119,8,24]{1,0,3,2:T(8,128)(2,1)} reshape(bf16[7616,192]{0,1:T(8,128)(2,1)S(1)} %get-tuple-element.88) | data formatting | bytes 5849088 | tf_op jit(solution)/shard_map/reshape | solution.py:104
  159.2 14.0 %reshape.148 = bf16[64,119,8,24]{1,0,3,2:T(8,128)(2,1)S(1)} reshape(bf16[7616,192]{0,1:T(8,128)(2,1)} %get-tuple-element.89) | data formatting | bytes 5849088 | tf_op jit(solution)/shard_map/reshape | solution.py:103
  173.2 21.7 %fusion.56 = (f32[64,8,119]{2,1,0:T(8,128)S(1)}, f32[64,8,119,119]{2,3,1,0:T(8,128)}) fusion(bf16[64,119,8,24]{1,0,3,2:T(8,128)(2,1)} %reshape.149, bf16[64,119,8,24]{1,0,3,2:T(8,128)(2,1)S(1)} %reshape.148, pred[64,119]{1,0:T(8,128)(4,1)S(1)} %compare_or_fusion), kind=kOutput, calls=%fused_computation.121 | convolution fusion | flops 369711104 | bytes 35102144 | tf_op jit(solution)/shard_map/slhe,smhe->shlm/dot_general | solution.py:91
  195.0 14.8 %fusion.1 = f32[64,8,119]{2,1,0:T(8,128)} fusion(f32[64,8,119,119]{2,3,1,0:T(8,128)} %get-tuple-element.108, f32[64,8,119]{2,1,0:T(8,128)S(1)} %get-tuple-element.107), kind=kLoop, calls=%fused_computation.6 | loop fusion | flops 14439936 | bytes 29489152 | tf_op jit(solution)/shard_map/reduce_sum | solution.py:109
  209.8 16.4 %convert_bitcast_fusion.1 = bf16[64,119,8,24]{1,3,2,0:T(8,128)(2,1)} fusion(f32[64,8,119,119]{2,3,1,0:T(8,128)} %get-tuple-element.108, f32[64,8,119]{2,1,0:T(8,128)} %fusion.1, f32[64,8,119]{2,1,0:T(8,128)S(1)} %get-tuple-element.107, bf16[64,119,8,24]{1,0,3,2:T(8,128)(2,1)S(1)} %copy-done.8), kind=kOutput, calls=%fused_computation.50 | convolution fusion | flops 371234304 | bytes 35338240 | tf_op jit(solution)/shard_map/shlm,smhe->slhe/dot_general | solution.py:112
  250.8 10.1 %multiply_convert_fusion.2 = (bf16[7616,256]{1,0:T(8,128)(2,1)S(1)}, bf16[7616,256]{1,0:T(8,128)(2,1)S(1)}, bf16[7616,256]{1,0:T(8,128)(2,1)}) fusion(f32[7616,512]{1,0:T(8,128)} %convolution_add_fusion, bf16[7616,192]{0,1:T(8,128)(2,1)S(1)} %copy-done.11, bf16[256,192]{1,0:T(8,128)(2,1)S(1)} %copy-done.22), kind=kOutput, calls=%fused_computation.22 | convolution fusion | flops 777928704 | bytes 30318592 | tf_op jit(solution)/shard_map/dot_general | solution.py:28
  266.4 34.8 %fusion = f32[16,512]{1,0:T(8,128)S(1)} fusion(f32[192,512]{1,0:T(8,128)} %fusion.34), kind=kCustom, calls=%all-reduce-scatter | all-reduce-scatter fusion | flops 131073 | bytes 426496
  327.3 13.8 %reshape.152 = bf16[64,119,8,24]{1,0,3,2:T(8,128)(2,1)S(1)} reshape(bf16[7616,192]{0,1:T(8,128)(2,1)} %convolution_convert_fusion) | data formatting | bytes 5849088 | tf_op jit(solution)/shard_map/reshape | solution.py:158
  341.1 16.1 %convert_bitcast_fusion = bf16[64,119,8,24]{1,3,2,0:T(8,128)(2,1)} fusion(f32[64,8,119,119]{2,3,1,0:T(8,128)} %get-tuple-element.108, f32[64,8,119]{2,1,0:T(8,128)S(1)} %log_add_fusion, bf16[64,119,8,24]{1,0,3,2:T(8,128)(2,1)S(1)} %reshape.152), kind=kOutput, calls=%fused_computation.49 | convolution fusion | flops 363983872 | bytes 35094528 | tf_op jit(solution)/shard_map/shlm,slhe->smhe/dot_general | solution.py:161
  357.2 30.9 %multiply_reduce_fusion = (f32[64,8,119]{2,1,0:T(8,128)}, f32[64,8,119,119]{2,3,1,0:T(8,128)}) fusion(f32[64,8,119,119]{2,3,1,0:T(8,128)} %get-tuple-element.108, f32[64,8,119]{2,1,0:T(8,128)S(1)} %log_add_fusion, bf16[64,119,8,24]{1,0,3,2:T(8,128)(2,1)} %reshape.147, bf16[64,119,8,24]{1,0,3,2:T(8,128)(2,1)S(1)} %reshape.152), kind=kOutput, calls=%fused_computation.1 | convolution fusion | flops 369711104 | bytes 64339968 | tf_op jit(solution)/shard_map/slhe,smhe->shlm/dot_general | solution.py:164
  388.1 26.4 %multiply_convert_fusion = bf16[64,8,119,119]{2,3,1,0:T(8,128)(2,1)} fusion(f32[64,8,119,119]{2,3,1,0:T(8,128)} %get-tuple-element.113, f32[64,8,119,119]{2,3,1,0:T(8,128)} %get-tuple-element.108, f32[64,8,119]{2,1,0:T(8,128)} %get-tuple-element.112, f32[64,8,119]{2,1,0:T(8,128)S(1)} %log_add_fusion), kind=kLoop, calls=%fused_computation | loop fusion | flops 29001728 | bytes 72991744 | tf_op jit(solution)/shard_map/convert_element_type | solution.py:165
  414.5 13.3 %fusion.12 = bf16[64,119,8,24]{1,3,2,0:T(8,128)(2,1)} fusion(bf16[64,8,119,119]{2,3,1,0:T(8,128)(2,1)} %multiply_convert_fusion, bf16[64,119,8,24]{1,0,3,2:T(8,128)(2,1)S(1)} %copy-done.3), kind=kOutput, calls=%fused_computation.47 | convolution fusion | flops 350945280 | bytes 20349952 | tf_op jit(solution)/shard_map/shlm,slhe->smhe/dot_general | solution.py:172
  427.8 12.9 %fusion.11 = bf16[64,119,8,24]{1,3,2,0:T(8,128)(2,1)} fusion(bf16[64,8,119,119]{2,3,1,0:T(8,128)(2,1)} %multiply_convert_fusion, bf16[64,119,8,24]{1,0,3,2:T(8,128)(2,1)S(1)} %copy-done.4), kind=kOutput, calls=%fused_computation.46 | convolution fusion | flops 350945280 | bytes 20349952 | tf_op jit(solution)/shard_map/shlm,smhe->slhe/dot_general | solution.py:169
  493.3 10.8 %multiply_reduce_fusion.3 = (f32[192]{0:T(256)S(1)}, f32[7616]{0:T(1024)S(1)}, f32[7616]{0:T(1024)S(1)}, f32[192]{0:T(256)S(1)}, f32[7616,192]{0,1:T(8,128)}) fusion(f32[7616,192]{0,1:T(8,128)} %reshape.157, f32[7616]{0:T(1024)S(1)} %copy-done.29, f32[7616]{0:T(1024)S(1)} %copy-done.27, f32[192]{0:T(256)S(1)} %copy-done.51, ...), kind=kOutput, calls=%fused_computation.34 | convolution fusion | flops 1698345472 | bytes 20817152 | tf_op jit(solution)/shard_map/dot_general | solution.py:28
  504.1 12.0 %convert_element_type.109 = f32[7616,576]{0,1:T(8,128)} convert(bf16[7616,576]{0,1:T(8,128)(2,1)} %copy-done.7) | non-fusion elementwise | flops 4386816 | bytes 26320896 | tf_op jit(solution)/shard_map/convert_element_type | solution.py:179
  532.3 30.3 %all-reduce.2 = f32[2048]{0:T(1024)S(1)} all-reduce(f32[2048]{0:T(1024)S(1)} %concatenate.22), channel_id=5, replica_groups=mesh['wide'=16,'narrow'=2] {'wide'}, use_global_device_ids=true, to_apply=%region_27.28.clone | all-reduce | flops 2048 | bytes 16384
  576.7 57.4 %reduce-scatter.4.cloned.1.call-done = f32[16,192]{1,0:T(8,128)} async-done(((f32[256,192]{1,0:T(8,128)}), f32[16,192]{1,0:T(8,128)}) %reduce-scatter.4.cloned.1.call-update) | async-done | bytes 12304 | tf_op jit(solution)/shard_map/reduce_scatter | solution.py:208
  641.1 13.8 %reshape.150 = bf16[64,119,192]{1,0,2:T(8,128)(2,1)S(1)} reshape(bf16[7616,192]{0,1:T(8,128)(2,1)} %fusion.9) | data formatting | bytes 5849088 | tf_op jit(solution)/shard_map/reshape | solution.py:128
  658.7 13.9 %reshape.156 = bf16[64,119,192]{1,0,2:T(8,128)(2,1)S(1)} reshape(bf16[7616,192]{0,1:T(8,128)(2,1)} %add_convert_fusion.1) | data formatting | bytes 5849088 | tf_op jit(solution)/shard_map/reshape | solution.py:186
  (220 shorter events, 200.0 us)
Async XLA Ops:
  7.2 31.2 %copy-start.5 = (bf16[64,119,192]{1,2,0:T(8,128)(2,1)S(1)}, bf16[64,119,192]{1,2,0:T(8,128)(2,1)}, u32[]{:S(2)}) copy-start(bf16[64,119,192]{1,2,0:T(8,128)(2,1)} %param.15) | copy-start | bytes 8773636
  7.2 568.1 %all-reduce.8.cloned.1.call-start = ((), (), s32[]{:S(2)}) async-start(), calls=%async_computation.2 | async-start | bytes 1572864
  145.3 27.8 %copy-start.44 = (s32[64,119]{1,0:T(8,128)S(1)}, s32[64,119]{1,0:T(8,128)}, u32[]{:S(2)}) copy-start(s32[64,119]{1,0:T(8,128)} %param.16) | copy-start | bytes 91396
  145.3 27.8 %copy-start.58 = (pred[119]{0:T(512)(128)(4,1)S(1)}, pred[119]{0:T(512)(128)(4,1)}, u32[]{:S(2)}) copy-start(pred[119]{0:T(512)(128)(4,1)} %iota_compare_fusion) | copy-start | bytes 361
  173.2 21.8 %copy-start.2 = (bf16[64,119,8,24]{1,0,3,2:T(8,128)(2,1)}, bf16[64,119,8,24]{1,0,3,2:T(8,128)(2,1)S(1)}, u32[]{:S(2)}) copy-start(bf16[64,119,8,24]{1,0,3,2:T(8,128)(2,1)S(1)} %reshape.148) | copy-start | bytes 8773636
  241.4 19.5 %copy-start = (f32[7616,192]{0,1:T(8,128)}, f32[7616,192]{0,1:T(8,128)S(1)}, u32[]{:S(2)}) copy-start(f32[7616,192]{0,1:T(8,128)S(1)} %get-tuple-element.110) | copy-start | bytes 17547268
  301.3 262.0 %collective-permute-start.2 = (f32[16,512]{1,0:T(8,128)S(1)}, f32[16,512]{1,0:T(8,128)}, u32[]{:S(2)}, u32[]{:S(2)}) collective-permute-start(f32[16,512]{1,0:T(8,128)S(1)} %fusion), channel_id=1, source_target_pairs={{0,6},{2,8},{4,10},{6,12},{8,14},{10,16},{12,18},{14,20},{16,22},{... | collective-permute-start | bytes 98312
  303.1 260.1 %collective-permute-start.1 = (f32[16,512]{1,0:T(8,128)S(1)}, f32[16,512]{1,0:T(8,128)}, u32[]{:S(2)}, u32[]{:S(2)}) collective-permute-start(f32[16,512]{1,0:T(8,128)S(1)} %fusion), channel_id=1, source_target_pairs={{0,4},{2,6},{4,8},{6,10},{8,12},{10,14},{12,16},{14,18},{16,20},{1... | collective-permute-start | bytes 98312
  305.0 258.3 %collective-permute-start = (f32[16,512]{1,0:T(8,128)S(1)}, f32[16,512]{1,0:T(8,128)}, u32[]{:S(2)}, u32[]{:S(2)}) collective-permute-start(f32[16,512]{1,0:T(8,128)S(1)} %fusion), channel_id=1, source_target_pairs={{0,2},{2,4},{4,6},{6,8},{8,10},{10,12},{12,14},{14,16},{16,18},{18... | collective-permute-start | bytes 98312
  307.6 255.7 %collective-permute-start.3 = (f32[12,512]{1,0:T(8,128)}, f32[12,512]{1,0:T(8,128)}, u32[]{:S(2)}, u32[]{:S(2)}) collective-permute-start(f32[12,512]{1,0:T(8,128)} %slice.120), channel_id=1, source_target_pairs={{0,8},{2,10},{4,12},{6,14},{8,16},{10,18},{12,20},{14,22},{16,24},... | collective-permute-start | bytes 73736
  388.1 26.4 %copy-start.3 = (bf16[64,119,8,24]{1,0,3,2:T(8,128)(2,1)S(1)}, bf16[64,119,8,24]{1,0,3,2:T(8,128)(2,1)}, u32[]{:S(2)}) copy-start(bf16[64,119,8,24]{1,0,3,2:T(8,128)(2,1)} %copy-done.2) | copy-start | bytes 8773636
  484.3 149.9 %reduce-scatter.4.cloned.1.call-start = ((), (), s32[]{:S(2)}) async-start(), calls=%async_computation.1 | async-start | bytes 278528 | tf_op jit(solution)/shard_map/reduce_scatter | solution.py:208
  488.8 187.4 %all-reduce.10.cloned.1.call-start = ((), (), s32[]{:S(2)}) async-start(), calls=%async_computation.3 | async-start | bytes 197632 | tf_op jit(solution)/shard_map/psum | solution.py:204
  522.2 112.0 %copy-start.23 = (bf16[256,192]{1,0:T(8,128)(2,1)S(1)}, bf16[256,192]{1,0:T(8,128)(2,1)}, u32[]{:S(2)}) copy-start(bf16[256,192]{1,0:T(8,128)(2,1)} %all_gather.18) | copy-start | bytes 294916
  522.2 112.0 %copy-start.47 = (f32[192]{0:T(256)S(1)}, f32[192]{0:T(256)}, u32[]{:S(2)}) copy-start(f32[192]{0:T(256)} %get-tuple-element.97) | copy-start | bytes 2308
  658.6 18.9 %copy-start.39 = (f32[16,192]{1,0:T(8,128)S(1)}, f32[16,192]{1,0:T(8,128)}, u32[]{:S(2)}) copy-start(f32[16,192]{1,0:T(8,128)} %param.20) | copy-start | bytes 36868
  658.6 18.9 %copy-start.45 = (f32[16,192]{1,0:T(8,128)S(1)}, f32[16,192]{1,0:T(8,128)}, u32[]{:S(2)}) copy-start(f32[16,192]{1,0:T(8,128)} %param.26) | copy-start | bytes 36868
  658.6 18.9 %copy-start.46 = (f32[16,192]{1,0:T(8,128)S(1)}, f32[16,192]{1,0:T(8,128)}, u32[]{:S(2)}) copy-start(f32[16,192]{1,0:T(8,128)} %param.27) | copy-start | bytes 36868
  658.6 20.2 %copy-start.25 = (f32[4,12,192]{2,0,1:T(4,128)S(1)}, f32[4,12,192]{2,0,1:T(4,128)}, u32[]{:S(2)}) copy-start(f32[4,12,192]{2,0,1:T(4,128)} %param.18) | copy-start | bytes 110596
  658.6 20.2 %copy-start.40 = (f32[4,12,192]{2,0,1:T(4,128)S(1)}, f32[4,12,192]{2,0,1:T(4,128)}, u32[]{:S(2)}) copy-start(f32[4,12,192]{2,0,1:T(4,128)} %param.22) | copy-start | bytes 110596
  658.6 20.2 %copy-start.41 = (f32[4,12,192]{2,0,1:T(4,128)S(1)}, f32[4,12,192]{2,0,1:T(4,128)}, u32[]{:S(2)}) copy-start(f32[4,12,192]{2,0,1:T(4,128)} %param.23) | copy-start | bytes 110596
  658.6 21.7 %copy-start.31 = (f32[12,512]{1,0:T(8,128)S(1)}, f32[12,512]{1,0:T(8,128)}, u32[]{:S(2)}) copy-start(f32[12,512]{1,0:T(8,128)} %param.19) | copy-start | bytes 73732
  658.6 21.7 %copy-start.42 = (f32[12,512]{1,0:T(8,128)S(1)}, f32[12,512]{1,0:T(8,128)}, u32[]{:S(2)}) copy-start(f32[12,512]{1,0:T(8,128)} %param.24) | copy-start | bytes 73732
  658.6 21.7 %copy-start.43 = (f32[12,512]{1,0:T(8,128)S(1)}, f32[12,512]{1,0:T(8,128)}, u32[]{:S(2)}) copy-start(f32[12,512]{1,0:T(8,128)} %param.25) | copy-start | bytes 73732
  (46 other events, 350.6 us)
Sparse Core Ops, SparseCore 0:
  484.4 90.8 all-reduce.7
  579.8 54.2 reduce-scatter.3
  637.9 19.8 all-reduce.9
where the time goes:
time: 697 us; the launch traced here: 688 us
  local copies, waits for them, and re-layouts  183 us (26%)
  matrix products  180 us (26%)
  blocking collectives  145 us (21%)
  other arithmetic  90.3 us (13%)
  waiting for transfers between devices  65.4 us (9%)
  between operations  16.6 us (2%)
  starting transfers between devices  8.09 us (1%)
    dot_general x12, matrix products, matmul(): return jnp.dot(left_term, right_term, preferred_element_type=jnp.float32)  68.3 us
    unnamed x2, blocking collectives  65.1 us
    reduce_scatter x1, waiting for transfers between devices, on_device(): lax.psum_scatter(summed[2], 'wide', scatter_dimension=0, tiled=True)  57.4 us
    dot_general x1, matrix products, on_device(): jnp.einsum('slhe,smhe->shlm', dmixed, valued, preferred_element_type=jnp....  30.9 us
    unnamed x139, local copies, waits for them, and re-layouts  29.6 us
    convert_element_type x1, other arithmetic, on_device(): (probs_b * (d_probs - jnp.sum(probs_b * d_probs, -1, keepdims=True))).ast...  26.4 us
    all_gather x1, blocking collectives, on_device(): lax.all_gather(master[3], 'wide', axis=0, tiled=True)  23 us
    dot_general x1, matrix products, scores_of(): jnp.einsum('slhe,smhe->shlm', query, keyed, preferred_element_type=jnp.fl...  21.7 us
  transfers between devices with their start and end apart: 7, of which 2 were waited for; matrix products, arithmetic and copies ran while one was open for 39% of the time, Pallas kernels for 0%

commit v1 on v0

v1 whole, which is shorter than its diff:
```python
import functools
import jax
import jax.numpy as jnp
from jax import lax
from jax.experimental import pallas as pl
from jax.experimental.pallas import tpu as pltpu
from jax.sharding import PartitionSpec as P

H = 8
FH = 256
STEP = 10
LANES = 128
F32 = jnp.float32
BF16 = jnp.bfloat16
NN = (((1,), (0,)), ((), ()))
NT = (((1,), (1,)), ((), ()))


def mm(a, b, dims=NN):
    return lax.dot_general(a, b, dims, preferred_element_type=F32)


def layer_kernel(
    group,
    x_ref, mask_ref, g_ref, wqkv_ref, wo_ref, w1_ref, w2_ref, vec_ref,
    y_ref, dx_ref, gqkv_ref, go_ref, g1_ref, g2_ref, gln_ref,
    wqkvt, wot, w1t, w2t, cols, n1a, n2a, oa, ha, e_s, ln_acc,
):
    step = pl.program_id(0)
    length = x_ref.shape[2]
    width = x_ref.shape[1]
    head = width // H
    tokens = group * LANES
    factor = float(head) ** (-0.5)
    log2e = 1.4426950408889634

    @pl.when(step == 0)
    def _():
        def aug(w, bias):
            rows = lax.broadcasted_iota(jnp.int32, (64, w.shape[1]), 0)
            tail = jnp.where(rows == 0, jnp.broadcast_to(bias, (64, w.shape[1])), 0.0)
            return jnp.concatenate([w.astype(F32), tail], axis=0).T.astype(BF16)

        zero_row = jnp.zeros((1, width), F32)
        v = vec_ref[...]
        piece = lambda i: v[:, i * width : (i + 1) * width]
        bias_qkv = jnp.concatenate([piece(2), zero_row, piece(3)], axis=1)
        wqkvt[...] = aug(wqkv_ref[...], bias_qkv)
        wot[...] = aug(wo_ref[...], piece(4))
        w1t[...] = aug(w1_ref[...], v[:, 8 * width : 8 * width + 2 * FH])
        w2t[...] = w2_ref[...].astype(F32).T.astype(BF16)
        for j, i in enumerate((0, 1, 5, 6, 7)):
            cols[j] = jnp.broadcast_to(piece(i), (LANES, width)).T
        rows = lax.broadcasted_iota(jnp.int32, (64, tokens), 0)
        one = jnp.where(rows == 0, 1.0, 0.0).astype(BF16)
        n1a[width:, :] = one
        n2a[width:, :] = one
        oa[width:, :] = one
        ha[FH:, :] = one[:16]
        gqkv_ref[...] = jnp.zeros_like(gqkv_ref)
        go_ref[...] = jnp.zeros_like(go_ref)
        g1_ref[...] = jnp.zeros_like(g1_ref)
        g2_ref[...] = jnp.zeros_like(g2_ref)
        ln_acc[...] = jnp.zeros_like(ln_acc)

    def wide(ref, g):
        t = ref[g]
        return jnp.concatenate([t, jnp.zeros((width, LANES - length), t.dtype)], axis=1)

    def tile(col):
        return jnp.concatenate([col] * group, axis=1) if group > 1 else col

    def norm(value):
        center = value - jnp.sum(value, 0, keepdims=True) * (1.0 / width)
        rstd = lax.rsqrt(jnp.sum(center * center, 0, keepdims=True) * (1.0 / width) + 1e-05)
        return center * rstd, rstd

    def norm_back(dn, xhat, rstd, gain, which):
        prod = dn * xhat
        a0, a1 = ln_acc[2 * which], ln_acc[2 * which + 1]
        for g in range(group):
            sl = slice(g * LANES, (g + 1) * LANES)
            a0 = a0 + prod[:, sl]
            a1 = a1 + dn[:, sl]
        ln_acc[2 * which] = a0
        ln_acc[2 * which + 1] = a1
        t = dn * gain
        m1 = jnp.sum(t, 0, keepdims=True) * (1.0 / width)
        m2 = jnp.sum(t * xhat, 0, keepdims=True) * (1.0 / width)
        return rstd * (t - m1 - xhat * m2)

    gain1, bias1, gain2, bias2, bias_c2 = (tile(cols[j]) for j in range(5))

    x = jnp.concatenate([wide(x_ref, g) for g in range(group)], axis=1).astype(F32)
    xhat1, rstd1 = norm(x)
    n1a[:width, :] = (xhat1 * gain1 + bias1).astype(BF16)
    qkv = mm(wqkvt[...], n1a[...])

    sub = lax.broadcasted_iota(jnp.int32, (8, LANES), 0)
    lane = lax.broadcasted_iota(jnp.int32, (8, LANES), 1)
    tile_q = jnp.where(sub == 0, 1.0, 0.0)
    tile_v = jnp.where(sub < 2, 1.0, 0.0)
    zeros = jnp.zeros((32, LANES), BF16)

    def padded(rows, tail):
        return jnp.concatenate([rows, tail], axis=0).astype(BF16)

    def pair_diag(a, b):
        return jnp.concatenate(
            [jnp.concatenate([a, zeros], axis=1), jnp.concatenate([zeros, b], axis=1)], axis=0
        )

    kept = []
    mixed = []
    for g in range(group):
        sl = slice(g * LANES, (g + 1) * LANES)
        m = mask_ref[pl.ds(step * group + g, 1), :]
        m = jnp.concatenate([m, jnp.zeros((1, LANES - length), jnp.int32)], axis=1)
        m8 = jnp.broadcast_to(m, (8, LANES))
        ok = (m8 != 0) | (lane == 0)
        tile_k = jnp.where((sub == 0) & jnp.logical_not(ok), -1e30, 0.0)
        mixed_rows = []
        for p in range(H // 2):
            qs, ks, vs = [], [], []
            for h in (2 * p, 2 * p + 1):
                r = slice(h * head, (h + 1) * head)
                qs.append(padded(qkv[r.start : r.stop, sl], tile_q))
                ks.append(padded(qkv[width + r.start : width + r.stop, sl], tile_k))
                vs.append(padded(qkv[2 * width + r.start : 2 * width + r.stop, sl], tile_v))
            qd = pair_diag(*qs)
            kp = jnp.concatenate(ks, axis=0)
            vp = jnp.concatenate(vs, axis=0)
            s = mm(kp.T, qd)
            top = jnp.max(s, 0, keepdims=True)
            e = jnp.exp2((s - top) * (factor * log2e)).astype(BF16)
            e_s[g, p] = e
            num = mm(vp, e)
            for j in range(2):
                part = num[32 * j : 32 * j + 32, j * LANES : (j + 1) * LANES]
                inv = 1.0 / part[head : head + 1]
                o = part[:head] * inv
                mixed_rows.append(o)
                kept.append((inv, o))
            kept[-1] = kept[-1] + (qd, kp, vp)
        mixed.append(jnp.concatenate(mixed_rows, axis=0))
    oa[:width, :] = jnp.concatenate(mixed, axis=1).astype(BF16)
    x1 = x + mm(wot[...], oa[...])
    xhat2, rstd2 = norm(x1)
    n2a[:width, :] = (xhat2 * gain2 + bias2).astype(BF16)
    z = mm(w1t[...], n2a[...])
    part_a, part_b = z[:FH], z[FH:]
    sigm = 1.0 / (1.0 + jnp.exp2(part_b * -log2e))
    silu = part_b * sigm
    ha[:FH, :] = (part_a * silu).astype(BF16)
    y = (x1 + mm(w2t[...], ha[:FH, :]) + bias_c2).astype(BF16)
    for g in range(group):
        y_ref[g] = y[:, g * LANES : g * LANES + length]

    gt = jnp.concatenate([wide(g_ref, g) for g in range(group)], axis=1)
    g2_ref[...] += mm(ha[...], gt, NT)
    dh = mm(w2_ref[...], gt)
    da = dh * silu
    db = dh * part_a * sigm * (1.0 + part_b * (1.0 - sigm))
    dz = jnp.concatenate([da, db], axis=0).astype(BF16)
    g1_ref[...] += mm(n2a[:208, :], dz, NT)
    dn2 = mm(w1_ref[...], dz)
    dx1 = gt.astype(F32) + norm_back(dn2, xhat2, rstd2, gain2, 1)
    da1 = dx1.astype(BF16)
    go_ref[...] += mm(oa[:208, :], da1, NT)
    do = mm(wo_ref[...], da1).astype(BF16).astype(F32)

    parts = []
    for g in range(group):
        sl = slice(g * LANES, (g + 1) * LANES)
        dqs, dks, dvs = [], [], []
        for p in range(H // 2):
            ds_ = []
            for j in range(2):
                h = 2 * p + j
                inv, o = kept[g * H + h][:2]
                d = do[h * head : (h + 1) * head, sl]
                low = jnp.sum(d * o, 0, keepdims=True) * -inv
                hi = low.astype(BF16).astype(F32)
                lo = low - hi
                tail = jnp.where(sub == 0, hi, jnp.where(sub == 1, lo, 0.0))
                ds_.append(padded(d * inv, tail))
            qd, kp, vp = kept[g * H + 2 * p + 1][2:]
            dd = pair_diag(*ds_)
            e = e_s[g, p]
            dpd = mm(vp.T, dd)
            dsc = (e.astype(F32) * dpd).astype(BF16)
            dv = mm(dd, e, NT)
            dq = mm(kp, dsc)
            dk = mm(qd, dsc, NT)
            for j in range(2):
                dqs.append(dq[32 * j : 32 * j + head, j * LANES : (j + 1) * LANES] * factor)
                dks.append(dk[32 * j : 32 * j + head] * factor)
                dvs.append(dv[32 * j : 32 * j + head])
        parts.append(jnp.concatenate(dqs + dks + dvs, axis=0))
    dqkv = jnp.concatenate(parts, axis=1).astype(BF16)
    gqkv_ref[...] += mm(n1a[:208, :], dqkv, NT)
    dn1 = mm(wqkv_ref[...], dqkv)
    dx = (dx1 + norm_back(dn1, xhat1, rstd1, gain1, 0)).astype(BF16)
    for g in range(group):
        dx_ref[g] = dx[:, g * LANES : g * LANES + length]

    @pl.when(step == pl.num_programs(0) - 1)
    def _():
        rows = [jnp.sum(ln_acc[i].T, 0, keepdims=True) for i in range(4)]
        gln_ref[...] = jnp.concatenate(rows + [jnp.zeros((4, width), F32)], axis=0)


def run_layer(x, mask, dout, wqkv, wo, w1, w2, vec, group=2):
    samples, width, length = x.shape
    tokens = group * LANES
    whole = lambda a: pl.BlockSpec(a.shape, lambda i: (0,) * a.ndim)
    per = pl.BlockSpec((group, width, length), lambda i: (i, 0, 0))
    const = lambda shape: pl.BlockSpec(shape, lambda i: (0,) * len(shape))
    shapes = [(208, 3 * width), (208, width), (208, 2 * FH), (272, width), (8, width)]
    return pl.pallas_call(
        functools.partial(layer_kernel, group),
        grid=(samples // group,),
        in_specs=[per, whole(mask), per, whole(wqkv), whole(wo), whole(w1), whole(w2), whole(vec)],
        out_specs=[per, per] + [const(s) for s in shapes],
        out_shape=[jax.ShapeDtypeStruct(x.shape, BF16)] * 2
        + [jax.ShapeDtypeStruct(s, F32) for s in shapes],
        scratch_shapes=[
            pltpu.VMEM((3 * width, 256), BF16),
            pltpu.VMEM((width, 256), BF16),
            pltpu.VMEM((2 * FH, 256), BF16),
            pltpu.VMEM((width, FH), BF16),
            pltpu.VMEM((5, width, LANES), F32),
            pltpu.VMEM((256, tokens), BF16),
            pltpu.VMEM((256, tokens), BF16),
            pltpu.VMEM((256, tokens), BF16),
            pltpu.VMEM((272, tokens), BF16),
            pltpu.VMEM((group, H // 2, LANES, 2 * LANES), BF16),
            pltpu.VMEM((4, width, LANES), F32),
        ],
        compiler_params=pltpu.CompilerParams(vmem_limit_bytes=60 * 1024 * 1024),
        name="layer",
    )(x, mask, dout, wqkv, wo, w1, w2, vec)


def adamw(weight, first_m, second_m, grad, decay):
    new_m = 0.9 * first_m + 0.1 * grad
    new_v = 0.999 * second_m + 0.001 * grad * grad
    ratio = new_m / (1.0 - 0.9**STEP) / (jnp.sqrt(new_v / (1.0 - 0.999**STEP)) + 1e-08)
    return (weight - 0.1 * (ratio + decay * weight), new_m, new_v)


def on_device(layer_input, mask, dout, attn_w, ffn_in, ffn_out, vec,
              m_attn, v_attn, m_in, v_in, m_out, v_out, m_vec, v_vec):
    width = layer_input.shape[2]
    n = lax.axis_size("wide")
    shard = (attn_w, ffn_in, ffn_out, vec)
    sizes = [a.size for a in shard]
    flat = jnp.concatenate([a.astype(BF16).reshape(-1) for a in shard])
    full = lax.all_gather(flat, "wide", axis=0, tiled=False)
    ends = [sum(sizes[:i]) for i in range(5)]
    cut = lambda i: full[:, ends[i] : ends[i + 1]]
    r = attn_w.shape[1]
    weights = cut(0).reshape(n, 4, r, width).transpose(1, 0, 2, 3).reshape(4, width, width)
    w1 = cut(1).reshape(width, 2 * FH)
    w2 = cut(2).reshape(FH, width)
    vector = cut(3).reshape(1, -1).astype(F32)
    wqkv = jnp.concatenate([weights[0], weights[1], weights[2]], axis=1)
    y, dx, gqkv, go, g1, g2, gln = run_layer(
        layer_input.transpose(0, 2, 1), mask, dout.transpose(0, 2, 1), wqkv, weights[3], w1, w2, vector
    )
    grad_attn = jnp.stack([gqkv[:width, :width], gqkv[:width, width : 2 * width], gqkv[:width, 2 * width :], go[:width]])
    grad_vec = jnp.concatenate([gln[0], gln[1], gqkv[width, :width], gqkv[width, 2 * width :], go[width],
                                gln[2], gln[3], g2[FH], g1[width]])
    parts = [
        grad_attn.reshape(4, n, r, width).transpose(1, 0, 2, 3).reshape(n, -1),
        g1[:width].reshape(n, -1),
        g2[:FH].reshape(n, -1),
        grad_vec.reshape(n, -1),
    ]
    packed = lax.psum(jnp.concatenate(parts, axis=1), "narrow")
    mine = lax.psum_scatter(packed, "wide", scatter_dimension=0, tiled=False)
    shares = [mine[ends[i] : ends[i + 1]].reshape(shard[i].shape) for i in range(4)]
    wa, ma, va = adamw(attn_w, m_attn, v_attn, shares[0], 0.01)
    wi, mi, vi = adamw(ffn_in, m_in, v_in, shares[1], 0.01)
    wo, mo, vo = adamw(ffn_out, m_out, v_out, shares[2], 0.01)
    wv, mv, vv = adamw(vec, m_vec, v_vec, shares[3], 0.0)
    return (y.transpose(0, 2, 1), dx.transpose(0, 2, 1), wa, ma, va, wi, mi, vi, wo, mo, vo, wv, mv, vv)


def solution(mesh):
    rows = P(("wide", "narrow"), None, None)
    states = [P(None, "wide", None), P("wide", None), P("wide", None), P("wide")]
    moments = [s for s in states for _ in range(2)]
    results = [s for s in states for _ in range(3)]
    return jax.shard_map(
        on_device,
        mesh=mesh,
        in_specs=tuple([rows, P(("wide", "narrow"), None), rows] + states + moments),
        out_specs=tuple([rows, rows] + results),
        check_vma=False,
    )
```

time: 697 us -> 321 us (0.46); the launches traced: 688 us -> 320 us
  matrix products: 180 us -> 0 us
  local copies, waits for them, and re-layouts: 183 us -> 16.1 us
  Pallas kernels: 0 us -> 145 us
  blocking collectives: 145 us -> 26.4 us
  other arithmetic: 90.3 us -> 8.1 us
  waiting for transfers between devices: 65.4 us -> 111 us
  starting transfers between devices: 8.09 us -> 0.08 us
    dot_general x18 -> x0, matrix products: 180 us -> none  [the longest x12 68.3 us: matmul(): return jnp.dot(left_term, right_term, preferred_element_type=jnp.float32)]
    pallas_call x0 -> x1, Pallas kernels: none -> 145 us  [run_layer(): pl.pallas_call(functools.partial(layer_kernel, group), grid=(samples // g...]
    reshape x10 -> x12, local copies, waits for them, and re-layouts: 109 us -> 3.33 us  [the longest x1 0.93 us: on_device(): w1 = cut(1).reshape(width, 2 * FH)]
    unnamed x8 -> x3, waiting for transfers between devices: 8.02 us -> 89.5 us
    unnamed x2 -> x0, blocking collectives: 65.1 us -> none
    reduce_scatter x1 -> x0, waiting for transfers between devices: 57.4 us -> none  [on_device(): lax.psum_scatter(summed[2], 'wide', scatter_dimension=0, tiled=True)]
    all_gather x4 -> x1, blocking collectives: 80.1 us -> 26.4 us  [on_device(): full = lax.all_gather(flat, 'wide', axis=0, tiled=False)]
    convert_element_type x6 -> x5, other arithmetic: 45.2 us -> 3.55 us  [the longest x4 2.95 us: on_device(): flat = jnp.concatenate([a.astype(BF16).reshape(-1) for a in shard])]
  transfers between devices with their start and end apart: 7 -> 2, of which waited for: 2 -> 2; matrix products, arithmetic and copies ran while one was open for 39% -> 0% of each run, Pallas kernels for 0% -> 0%
where the time goes in v1:
time: 321 us; the launch traced here: 320 us
  Pallas kernels  145 us (45%)
  waiting for transfers between devices  111 us (35%)
  blocking collectives  26.4 us (8%)
  local copies, waits for them, and re-layouts  16.1 us (5%)
  between operations  14.4 us (4%)
  other arithmetic  8.1 us (3%)
    pallas_call x1, Pallas kernels, run_layer(): pl.pallas_call(functools.partial(layer_kernel, group), grid=(samples // g...  145 us
    unnamed x3, waiting for transfers between devices  89.5 us
    all_gather x1, blocking collectives, on_device(): full = lax.all_gather(flat, 'wide', axis=0, tiled=False)  26.4 us
    psum x1, waiting for transfers between devices, on_device(): packed = lax.psum(jnp.concatenate(parts, axis=1), 'narrow')  21.2 us
  transfers between devices with their start and end apart: 2, of which 2 were waited for; matrix products, arithmetic and copies ran while one was open for 0% of the time, Pallas kernels for 0%

profile of v1, /device:TPU:0, one launch (start us, length us, event | category | flops | bytes accessed | tf_op | source)
XLA Modules:
  0.0 320.5 jit_solution(17022587074435939357)
XLA Ops:
  7.2 0.7 convert_element_type.20
  7.9 0.7 convert_element_type.19
  8.7 0.8 convert_element_type.18
  9.5 0.8 convert_element_type.17
  10.5 26.4 %all-gather.1 = bf16[16,1,18560]{2,1,0:T(2,128)(2,1)S(1)} all-gather(bf16[1,1,18560]{2,1,0:T(2,128)(2,1)S(1)} %reshape.122), channel_id=2, replica_groups=mesh['wide'=16,'narrow'=2] {'wide'}, dimensions={0}, use_global_device_ids=true | all-gather | bytes 631040 | tf_op jit(solution)/shard_map/all_gather | solution.py:259
  38.4 0.7 squeeze.42.wo_ref
  39.0 0.9 reshape.111.w1_ref
  40.0 0.8 reshape.112.w2_ref
  40.8 0.8 pad_maximum_fusion.1.wqkv_ref
  41.6 144.7 %layer.1 = (bf16[64,192,119]{2,1,0:T(8,128)(2,1)}, bf16[64,192,119]{2,1,0:T(8,128)(2,1)}, f32[208,576]{1,0:T(8,128)}, f32[208,192]{1,0:T(8,128)}, f32[208,512]{1...) custom-call(bf16[64,192,119]{2,1,0:T(8,128)(2,1)} %bitcast.38, s32[64,119]{1,0:T(8,128)} %mask_ref.1, ...), custom_call_target="tpu_custom_call" | custom-call | tf_op jit(solution)/shard_map/layer/pallas_call | solution.py:220
  186.3 0.8 slice.112
  187.1 1.0 slice.104
  188.1 0.7 slice.113
  188.8 1.0 slice.103
  191.1 1.1 pad_maximum_fusion
  193.4 89.5 %all-reduce.6.cloned.1.call-done = f32[16,18560]{1,0:T(8,128)} async-done(((f32[16,18560]{1,0:T(8,128)}), f32[16,18560]{1,0:T(8,128)}) %all-reduce.6.cloned.1.call-update) | async-done | bytes 1187856
  283.0 2.4 constant_dynamic-slice_fusion
  285.4 21.2 %all-reduce.4.cloned.1.call-done = f32[1,18560]{1,0:T(1,128)} async-done(((f32[1,18560]{1,0:T(1,128)}), f32[1,18560]{1,0:T(1,128)}) %all-reduce.4.cloned.1.call-update) | async-done | bytes 74256 | tf_op jit(solution)/shard_map/psum | solution.py:280
  306.6 0.9 slice_reduce_fusion
  307.6 0.7 copy.55
  309.6 0.8 slice_reduce_fusion.1
  310.4 0.7 slice_reduce_fusion.2
  311.2 0.7 multiply_subtract_fusion
  312.5 1.1 multiply_subtract_fusion.2
  (74 shorter events, 6.3 us)
Async XLA Ops:
  7.2 275.8 %all-reduce.6.cloned.1.call-start = ((), (), s32[]{:S(2)}) async-start(), calls=%async_computation.1 | async-start | bytes 2375680
  186.3 3.5 %copy-start.2 = (f32[208,192]{1,0:T(8,128)S(1)}, f32[208,192]{1,0:T(8,128)}, u32[]{:S(2)}) copy-start(f32[208,192]{1,0:T(8,128)} %get-tuple-element.24) | copy-start | bytes 479236
  186.3 3.6 %copy-start = (f32[208,576]{1,0:T(8,128)S(1)}, f32[208,576]{1,0:T(8,128)}, u32[]{:S(2)}) copy-start(f32[208,576]{1,0:T(8,128)} %get-tuple-element.23) | copy-start | bytes 1437700
  188.0 1.9 copy-start.11
  192.2 0.7 copy-start.15
  192.2 115.3 %copy-start.1 = (f32[4,12,192]{2,0,1:T(4,128)S(1)}, f32[4,12,192]{2,0,1:T(4,128)}, u32[]{:S(2)}) copy-start(f32[4,12,192]{2,0,1:T(4,128)} %param.18) | copy-start | bytes 110596
  192.2 115.3 %copy-start.5 = (f32[4,12,192]{2,0,1:T(4,128)S(1)}, f32[4,12,192]{2,0,1:T(4,128)}, u32[]{:S(2)}) copy-start(f32[4,12,192]{2,0,1:T(4,128)} %param.22) | copy-start | bytes 110596
  192.2 115.3 %copy-start.6 = (f32[4,12,192]{2,0,1:T(4,128)S(1)}, f32[4,12,192]{2,0,1:T(4,128)}, u32[]{:S(2)}) copy-start(f32[4,12,192]{2,0,1:T(4,128)} %param.23) | copy-start | bytes 110596
  192.2 119.0 %copy-start.3 = (f32[12,512]{1,0:T(8,128)S(1)}, f32[12,512]{1,0:T(8,128)}, u32[]{:S(2)}) copy-start(f32[12,512]{1,0:T(8,128)} %param.19) | copy-start | bytes 73732
  192.2 119.0 %copy-start.7 = (f32[12,512]{1,0:T(8,128)S(1)}, f32[12,512]{1,0:T(8,128)}, u32[]{:S(2)}) copy-start(f32[12,512]{1,0:T(8,128)} %param.24) | copy-start | bytes 73732
  192.2 119.0 %copy-start.8 = (f32[12,512]{1,0:T(8,128)S(1)}, f32[12,512]{1,0:T(8,128)}, u32[]{:S(2)}) copy-start(f32[12,512]{1,0:T(8,128)} %param.25) | copy-start | bytes 73732
  192.3 119.6 %copy-start.4 = (f32[16,192]{1,0:T(8,128)S(1)}, f32[16,192]{1,0:T(8,128)}, u32[]{:S(2)}) copy-start(f32[16,192]{1,0:T(8,128)} %param.20) | copy-start | bytes 36868
  192.3 119.6 %copy-start.9 = (f32[16,192]{1,0:T(8,128)S(1)}, f32[16,192]{1,0:T(8,128)}, u32[]{:S(2)}) copy-start(f32[16,192]{1,0:T(8,128)} %param.26) | copy-start | bytes 36868
  192.3 119.6 %copy-start.10 = (f32[16,192]{1,0:T(8,128)S(1)}, f32[16,192]{1,0:T(8,128)}, u32[]{:S(2)}) copy-start(f32[16,192]{1,0:T(8,128)} %param.27) | copy-start | bytes 36868
  192.3 120.2 %copy-start.12 = (f32[128]{0:T(128)S(1)}, f32[128]{0:T(128)}, u32[]{:S(2)}) copy-start(f32[128]{0:T(128)} %param.21) | copy-start | bytes 1540
  192.3 120.2 %copy-start.13 = (f32[128]{0:T(128)S(1)}, f32[128]{0:T(128)}, u32[]{:S(2)}) copy-start(f32[128]{0:T(128)} %param.28) | copy-start | bytes 1540
  192.3 120.2 %copy-start.14 = (f32[128]{0:T(128)S(1)}, f32[128]{0:T(128)}, u32[]{:S(2)}) copy-start(f32[128]{0:T(128)} %param.29) | copy-start | bytes 1540
  192.3 114.2 %all-reduce.4.cloned.1.call-start = ((), (), s32[]{:S(2)}) async-start(), calls=%async_computation | async-start | bytes 148480 | tf_op jit(solution)/shard_map/psum | solution.py:280
Sparse Core Ops, SparseCore 0:
  192.5 90.4 all-reduce.5
  285.5 21.0 all-reduce.3

commit v2 on v1

--- a/solution.py
+++ b/solution.py
@@ -10,6 +10,7 @@
 FH = 256
 STEP = 10
 LANES = 128
+GROUP = 2
 F32 = jnp.float32
 BF16 = jnp.bfloat16
 NN = (((1,), (0,)), ((), ()))
@@ -22,9 +23,11 @@
 
 def layer_kernel(
     group,
-    x_ref, mask_ref, g_ref, wqkv_ref, wo_ref, w1_ref, w2_ref, vec_ref,
-    y_ref, dx_ref, gqkv_ref, go_ref, g1_ref, g2_ref, gln_ref,
-    wqkvt, wot, w1t, w2t, cols, n1a, n2a, oa, ha, e_s, ln_acc,
+    x_ref, mask_ref, g_ref, full_ref,
+    y_ref, dx_ref, packed_ref,
+    big, w2f, vec_s, wqkv_ref, wo_ref, w1_ref, w2_ref,
+    wqkvt, wot, w1t, w2t, cols, n1a, n2a, oa, ha, e_s,
+    gqkv_ref, go_ref, g1_ref, g2_ref, ln_acc, pack_s,
 ):
     step = pl.program_id(0)
     length = x_ref.shape[2]
@@ -36,13 +39,29 @@
 
     @pl.when(step == 0)
     def _():
+        shards, block_rows, _ = full_ref.shape
+        depth = width // shards
+        extra = block_rows - depth
+        per_vec = vec_s.shape[1] // shards
+        for w in range(shards):
+            block = full_ref[w].astype(F32)
+            big[w * depth : (w + 1) * depth, :] = block[:depth]
+            for j in range(4):
+                at = (4 * w + j) * extra
+                w2f[at : at + extra, :] = block[depth:, j * width : (j + 1) * width]
+            vec_s[:, w * per_vec : (w + 1) * per_vec] = block[depth : depth + 1, 4 * width : 4 * width + per_vec]
+        wqkv_ref[...] = big[:, : 3 * width].astype(BF16)
+        wo_ref[...] = big[:, 3 * width : 4 * width].astype(BF16)
+        w1_ref[...] = big[:, 4 * width :].astype(BF16)
+        w2_ref[...] = w2f[...].astype(BF16)
+
         def aug(w, bias):
             rows = lax.broadcasted_iota(jnp.int32, (64, w.shape[1]), 0)
             tail = jnp.where(rows == 0, jnp.broadcast_to(bias, (64, w.shape[1])), 0.0)
             return jnp.concatenate([w.astype(F32), tail], axis=0).T.astype(BF16)
 
         zero_row = jnp.zeros((1, width), F32)
-        v = vec_ref[...]
+        v = vec_s[...]
         piece = lambda i: v[:, i * width : (i + 1) * width]
         bias_qkv = jnp.concatenate([piece(2), zero_row, piece(3)], axis=1)
         wqkvt[...] = aug(wqkv_ref[...], bias_qkv)
@@ -207,24 +226,47 @@
     @pl.when(step == pl.num_programs(0) - 1)
     def _():
         rows = [jnp.sum(ln_acc[i].T, 0, keepdims=True) for i in range(4)]
-        gln_ref[...] = jnp.concatenate(rows + [jnp.zeros((4, width), F32)], axis=0)
-
-
-def run_layer(x, mask, dout, wqkv, wo, w1, w2, vec, group=2):
+        vec = jnp.concatenate(
+            [rows[0], rows[1], gqkv_ref[width : width + 1, :width], gqkv_ref[width : width + 1, 2 * width :],
+             go_ref[width : width + 1], rows[2], rows[3], g2_ref[FH : FH + 1], g1_ref[width : width + 1]],
+            axis=1,
+        )
+        shards, block_rows, _ = packed_ref.shape
+        depth = width // shards
+        extra = block_rows - depth
+        per_vec = vec.shape[1] // shards
+        pack_s[...] = jnp.zeros_like(pack_s)
+        for w in range(shards):
+            r = slice(w * depth, (w + 1) * depth)
+            pack_s[w, :depth, : 4 * width] = jnp.concatenate([gqkv_ref[r, :], go_ref[r, :]], axis=1)
+            pack_s[w, :depth, 4 * width :] = g1_ref[r, :]
+            at = 4 * w * extra
+            pack_s[w, depth:, : 4 * width] = jnp.concatenate(
+                [g2_ref[at + j * extra : at + (j + 1) * extra, :] for j in range(4)], axis=1
+            )
+            pack_s[w, depth : depth + 1, 4 * width : 4 * width + per_vec] = vec[:, w * per_vec : (w + 1) * per_vec]
+        packed_ref[...] = pack_s[...].astype(BF16)
+
+
+def run_layer(x, mask, dout, full, group):
     samples, width, length = x.shape
     tokens = group * LANES
     whole = lambda a: pl.BlockSpec(a.shape, lambda i: (0,) * a.ndim)
     per = pl.BlockSpec((group, width, length), lambda i: (i, 0, 0))
-    const = lambda shape: pl.BlockSpec(shape, lambda i: (0,) * len(shape))
-    shapes = [(208, 3 * width), (208, width), (208, 2 * FH), (272, width), (8, width)]
     return pl.pallas_call(
         functools.partial(layer_kernel, group),
         grid=(samples // group,),
-        in_specs=[per, whole(mask), per, whole(wqkv), whole(wo), whole(w1), whole(w2), whole(vec)],
-        out_specs=[per, per] + [const(s) for s in shapes],
-        out_shape=[jax.ShapeDtypeStruct(x.shape, BF16)] * 2
-        + [jax.ShapeDtypeStruct(s, F32) for s in shapes],
+        in_specs=[per, whole(mask), per, whole(full)],
+        out_specs=[per, per, whole(full)],
+        out_shape=[jax.ShapeDtypeStruct(x.shape, BF16)] * 2 + [jax.ShapeDtypeStruct(full.shape, BF16)],
         scratch_shapes=[
+            pltpu.VMEM((width, 4 * width + 2 * FH), F32),
+            pltpu.VMEM((FH, width), F32),
+            pltpu.VMEM((1, 8 * width + 2 * FH), F32),
+            pltpu.VMEM((width, 3 * width), BF16),
+            pltpu.VMEM((width, width), BF16),
+            pltpu.VMEM((width, 2 * FH), BF16),
+            pltpu.VMEM((FH, width), BF16),
             pltpu.VMEM((3 * width, 256), BF16),
             pltpu.VMEM((width, 256), BF16),
             pltpu.VMEM((2 * FH, 256), BF16),
@@ -235,11 +277,133 @@
             pltpu.VMEM((256, tokens), BF16),
             pltpu.VMEM((272, tokens), BF16),
             pltpu.VMEM((group, H // 2, LANES, 2 * LANES), BF16),
+            pltpu.VMEM((208, 3 * width), F32),
+            pltpu.VMEM((208, width), F32),
+            pltpu.VMEM((208, 2 * FH), F32),
+            pltpu.VMEM((272, width), F32),
             pltpu.VMEM((4, width, LANES), F32),
+            pltpu.VMEM(full.shape, F32),
         ],
         compiler_params=pltpu.CompilerParams(vmem_limit_bytes=60 * 1024 * 1024),
         name="layer",
-    )(x, mask, dout, wqkv, wo, w1, w2, vec)
+    )(x, mask, dout, full)
+
+
+def send(src, dst, send_sem, recv_sem, device):
+    copy = pltpu.make_async_remote_copy(
+        src_ref=src, dst_ref=dst, send_sem=send_sem, recv_sem=recv_sem,
+        device_id=device, device_id_type=pl.DeviceIdType.MESH,
+    )
+    copy.start()
+    return copy
+
+
+def meet(devices):
+    barrier = pltpu.get_barrier_semaphore()
+    for device in devices:
+        pl.semaphore_signal(barrier, inc=1, device_id=device, device_id_type=pl.DeviceIdType.MESH)
+    pl.semaphore_wait(barrier, len(devices))
+
+
+def gather_kernel(n, attn_ref, w1_ref, w2_ref, vec_ref, out_ref, send1, recv1, send2, recv2):
+    me = lax.axis_index("wide")
+    core, chip, chips = lax.rem(me, 2), lax.div(me, 2), n // 2
+    peer = lambda k: 2 * lax.rem(chip + k, chips) + core
+    sibling = {"wide": me + 1 - 2 * core}
+    depth = attn_ref.shape[0]
+    width = attn_ref.shape[2]
+    extra = w2_ref.shape[0] // 4
+    lanes = out_ref.shape[2]
+    top = jnp.concatenate([attn_ref[:, i, :] for i in range(4)] + [w1_ref[...]], axis=1)
+    bottom = jnp.concatenate(
+        [w2_ref[j * extra : (j + 1) * extra, :] for j in range(4)]
+        + [jnp.broadcast_to(vec_ref[...], (extra, vec_ref.shape[1])),
+           jnp.zeros((extra, lanes - 4 * width - vec_ref.shape[1]), F32)],
+        axis=1,
+    )
+    out_ref[me] = jnp.concatenate([top, bottom], axis=0).astype(BF16)
+    meet([{"wide": peer(k)} for k in range(1, chips)] + [sibling])
+    mine = out_ref.at[me]
+    copies = [send(mine, mine, send1.at[k], recv1.at[k], {"wide": peer(k)}) for k in range(1, chips)]
+    passed = [send(mine, mine, send2.at[0], recv2.at[0], sibling)]
+    for k in range(1, chips):
+        copies[k - 1].wait_recv()
+        block = out_ref.at[peer(chips - k)]
+        passed.append(send(block, block, send2.at[k], recv2.at[k], sibling))
+    for copy in copies:
+        copy.wait_send()
+    for copy in passed:
+        copy.wait()
+
+
+def gather(attn, w1, w2, vec, n):
+    rows = attn.shape[0] + w2.shape[0] // 4
+    lanes = 4 * attn.shape[2] + w1.shape[1]
+    sems = pltpu.SemaphoreType.DMA((n // 2,))
+    return pl.pallas_call(
+        functools.partial(gather_kernel, n),
+        out_shape=jax.ShapeDtypeStruct((n, rows, lanes), BF16),
+        in_specs=[pl.BlockSpec(memory_space=pltpu.VMEM)] * 4,
+        out_specs=pl.BlockSpec(memory_space=pltpu.VMEM),
+        scratch_shapes=[sems] * 4,
+        compiler_params=pltpu.CompilerParams(collective_id=0, has_side_effects=True),
+        name="gather",
+    )(attn, w1, w2, vec)
+
+
+def reduce_kernel(n, copies_of, part_ref, out_ref, core_buf, sum_buf, wide_buf, narrow_buf,
+                  send0, recv0, send1, recv1, send2, recv2):
+    me, mine = lax.axis_index("wide"), lax.axis_index("narrow")
+    core, chip, chips = lax.rem(me, 2), lax.div(me, 2), n // 2
+    peer = lambda k: 2 * lax.rem(chip + k, chips) + core
+    sibling = {"wide": me + 1 - 2 * core}
+    twin = lambda j: {"narrow": lax.rem(mine + j, copies_of)}
+    meet([{"wide": peer(k)} for k in range(1, chips)] + [sibling] + [twin(j) for j in range(1, copies_of)])
+    order = list(range(1, chips)) + [0]
+    first = {}
+    for k in order:
+        other = peer(k) + 1 - 2 * core
+        first[k] = send(part_ref.at[other], core_buf.at[k], send0.at[k], recv0.at[k], sibling)
+    second = {}
+    for k in order:
+        first[k].wait_recv()
+        total = part_ref[peer(k)].astype(F32) + core_buf[k].astype(F32)
+        if k:
+            sum_buf[k] = total.astype(BF16)
+            second[k] = send(sum_buf.at[k], wide_buf.at[k], send1.at[k], recv1.at[k], {"wide": peer(k)})
+    for k in range(1, chips):
+        second[k].wait_recv()
+        total = total + wide_buf[k].astype(F32)
+    narrow_buf[mine] = total
+    third = [
+        send(narrow_buf.at[mine], narrow_buf.at[mine], send2.at[j], recv2.at[j], twin(j))
+        for j in range(1, copies_of)
+    ]
+    for copy in third:
+        copy.wait_recv()
+    result = narrow_buf[0]
+    for j in range(1, copies_of):
+        result = result + narrow_buf[j]
+    out_ref[...] = result
+    for copy in list(first.values()) + list(second.values()) + third:
+        copy.wait_send()
+
+
+def reduce_shares(packed, n, copies_of):
+    chips = n // 2
+    block = packed.shape[1:]
+    sems = pltpu.SemaphoreType.DMA((chips,))
+    few = pltpu.SemaphoreType.DMA((copies_of,))
+    return pl.pallas_call(
+        functools.partial(reduce_kernel, n, copies_of),
+        out_shape=jax.ShapeDtypeStruct(block, F32),
+        in_specs=[pl.BlockSpec(memory_space=pltpu.VMEM)],
+        out_specs=pl.BlockSpec(memory_space=pltpu.VMEM),
+        scratch_shapes=[pltpu.VMEM((chips,) + block, BF16)] * 3
+        + [pltpu.VMEM((copies_of,) + block, F32), sems, sems, sems, sems, few, few],
+        compiler_params=pltpu.CompilerParams(collective_id=1, has_side_effects=True),
+        name="reduce",
+    )(packed)
 
 
 def adamw(weight, first_m, second_m, grad, decay):
@@ -249,42 +413,48 @@
     return (weight - 0.1 * (ratio + decay * weight), new_m, new_v)
 
 
+def update_kernel(grad_ref, *refs):
+    ins, outs = refs[:12], refs[12:]
+    width = ins[0].shape[2]
+    depth = ins[0].shape[0]
+    extra = ins[6].shape[0] // 4
+
+    def step(base, index, grad, decay):
+        for ref, value in zip(outs[base : base + 3], adamw(*(r[index] for r in ins[base : base + 3]), grad, decay)):
+            ref[index] = value
+
+    for i in range(4):
+        step(0, (slice(None), i, slice(None)), grad_ref[:depth, i * width : (i + 1) * width], 0.01)
+    step(3, (slice(None), slice(None)), grad_ref[:depth, 4 * width :], 0.01)
+    for j in range(4):
+        step(6, (slice(j * extra, (j + 1) * extra), slice(None)), grad_ref[depth:, j * width : (j + 1) * width], 0.01)
+    per_vec = ins[9].shape[1]
+    step(9, (slice(None), slice(None)), grad_ref[depth : depth + 1, 4 * width : 4 * width + per_vec], 0.0)
+
+
+def update(grad, states):
+    vmem = pl.BlockSpec(memory_space=pltpu.VMEM)
+    return pl.pallas_call(
+        update_kernel,
+        out_shape=[jax.ShapeDtypeStruct(a.shape, F32) for a in states],
+        in_specs=[vmem] * 13,
+        out_specs=[vmem] * 12,
+        name="update",
+    )(grad, *states)
+
+
 def on_device(layer_input, mask, dout, attn_w, ffn_in, ffn_out, vec,
               m_attn, v_attn, m_in, v_in, m_out, v_out, m_vec, v_vec):
-    width = layer_input.shape[2]
-    n = lax.axis_size("wide")
-    shard = (attn_w, ffn_in, ffn_out, vec)
-    sizes = [a.size for a in shard]
-    flat = jnp.concatenate([a.astype(BF16).reshape(-1) for a in shard])
-    full = lax.all_gather(flat, "wide", axis=0, tiled=False)
-    ends = [sum(sizes[:i]) for i in range(5)]
-    cut = lambda i: full[:, ends[i] : ends[i + 1]]
-    r = attn_w.shape[1]
-    weights = cut(0).reshape(n, 4, r, width).transpose(1, 0, 2, 3).reshape(4, width, width)
-    w1 = cut(1).reshape(width, 2 * FH)
-    w2 = cut(2).reshape(FH, width)
-    vector = cut(3).reshape(1, -1).astype(F32)
-    wqkv = jnp.concatenate([weights[0], weights[1], weights[2]], axis=1)
-    y, dx, gqkv, go, g1, g2, gln = run_layer(
-        layer_input.transpose(0, 2, 1), mask, dout.transpose(0, 2, 1), wqkv, weights[3], w1, w2, vector
-    )
-    grad_attn = jnp.stack([gqkv[:width, :width], gqkv[:width, width : 2 * width], gqkv[:width, 2 * width :], go[:width]])
-    grad_vec = jnp.concatenate([gln[0], gln[1], gqkv[width, :width], gqkv[width, 2 * width :], go[width],
-                                gln[2], gln[3], g2[FH], g1[width]])
-    parts = [
-        grad_attn.reshape(4, n, r, width).transpose(1, 0, 2, 3).reshape(n, -1),
-        g1[:width].reshape(n, -1),
-        g2[:FH].reshape(n, -1),
-        grad_vec.reshape(n, -1),
-    ]
-    packed = lax.psum(jnp.concatenate(parts, axis=1), "narrow")
-    mine = lax.psum_scatter(packed, "wide", scatter_dimension=0, tiled=False)
-    shares = [mine[ends[i] : ends[i + 1]].reshape(shard[i].shape) for i in range(4)]
-    wa, ma, va = adamw(attn_w, m_attn, v_attn, shares[0], 0.01)
-    wi, mi, vi = adamw(ffn_in, m_in, v_in, shares[1], 0.01)
-    wo, mo, vo = adamw(ffn_out, m_out, v_out, shares[2], 0.01)
-    wv, mv, vv = adamw(vec, m_vec, v_vec, shares[3], 0.0)
-    return (y.transpose(0, 2, 1), dx.transpose(0, 2, 1), wa, ma, va, wi, mi, vi, wo, mo, vo, wv, mv, vv)
+    n, copies_of = lax.axis_size("wide"), lax.axis_size("narrow")
+    turn = lambda a: a.transpose(1, 0, 2)
+    row = lambda a: a.reshape(1, -1)
+    full = gather(turn(attn_w), ffn_in, ffn_out, row(vec), n)
+    y, dx, packed = run_layer(layer_input.transpose(0, 2, 1), mask, dout.transpose(0, 2, 1), full, GROUP)
+    share = reduce_shares(packed, n, copies_of)
+    new = update(share, [turn(attn_w), turn(m_attn), turn(v_attn), ffn_in, m_in, v_in, ffn_out, m_out, v_out,
+                         row(vec), row(m_vec), row(v_vec)])
+    return (y.transpose(0, 2, 1), dx.transpose(0, 2, 1), *(turn(a) for a in new[:3]), *new[3:9],
+            *(a.reshape(-1) for a in new[9:]))
 
 
 def solution(mesh):

time: 321 us -> 181 us (0.56)
  waiting for transfers between devices: 111 us -> 0 us
  Pallas kernels: 145 us -> 180 us
  blocking collectives: 26.4 us -> 0 us
  local copies, waits for them, and re-layouts: 16.1 us -> 0 us
  between operations: 14.4 us -> 0.66 us
  other arithmetic: 8.1 us -> 0 us
    unnamed x3 -> x0, waiting for transfers between devices: 89.5 us -> none
    pallas_call x0 -> x3, Pallas kernels: none -> 35.7 us  [the longest x1 18.6 us: reduce_shares(): pl.pallas_call(functools.partial(reduce_kernel, n, copies_of), out_shape=...]
    all_gather x1 -> x0, blocking collectives: 26.4 us -> none  [on_device(): full = lax.all_gather(flat, 'wide', axis=0, tiled=False)]
    psum x1 -> x0, waiting for transfers between devices: 21.2 us -> none  [on_device(): packed = lax.psum(jnp.concatenate(parts, axis=1), 'narrow')]
    slice x15 -> x0, local copies, waits for them, and re-layouts: 6.1 us -> none  [the longest x3 2.4 us: on_device(): mine[ends[i]:ends[i + 1]].reshape(shard[i].shape)]
    unnamed x39 -> x0, local copies, waits for them, and re-layouts: 5.59 us -> none
    convert_element_type x5 -> x0, other arithmetic: 3.55 us -> none  [the longest x4 2.95 us: on_device(): flat = jnp.concatenate([a.astype(BF16).reshape(-1) for a in shard])]
    reshape x12 -> x0, local copies, waits for them, and re-layouts: 3.33 us -> none  [the longest x1 0.93 us: on_device(): w1 = cut(1).reshape(width, 2 * FH)]
  transfers between devices with their start and end apart: 2 -> 0, of which waited for: 2 -> 0; matrix products, arithmetic and copies ran while one was open for 0% -> 0% of each run, Pallas kernels for 0% -> 0%
where the time goes in v2:
time: 181 us; the launch traced here: 180 us
  Pallas kernels  180 us (99%)
    pallas_call x1, Pallas kernels, run_layer(): pl.pallas_call(functools.partial(layer_kernel, group), grid=(samples // g...  144 us
    pallas_call x1, Pallas kernels, reduce_shares(): pl.pallas_call(functools.partial(reduce_kernel, n, copies_of), out_shape=...  18.6 us
    pallas_call x1, Pallas kernels, gather(): pl.pallas_call(functools.partial(gather_kernel, n), out_shape=jax.ShapeDt...  15.1 us

profile of v2, /device:TPU:0, one launch (start us, length us, event | category | flops | bytes accessed | tf_op | source)
XLA Modules:
  0.0 180.4 jit_solution(6257206894881552195)
XLA Ops:
  0.6 15.1 %gather.1.full_ref = bf16[16,16,1280]{2,1,0:T(8,128)(2,1)} custom-call(f32[12,4,192]{2,1,0:T(4,128)} %bitcast.18, f32[12,512]{1,0:T(8,128)} %refs_3_.1, f32[16,192]{1,0:T(8,128)} %refs_6_.1, f32[1,128]{1,0:T(1,128)} %bitcast.22), custom_call_target="tpu_custom_call" | custom-call | tf_op jit(solution)/shard_map/gather/pallas_call | solution.py:343
  15.8 144.0 %layer.1 = (bf16[64,192,119]{2,1,0:T(8,128)(2,1)}, bf16[64,192,119]{2,1,0:T(8,128)(2,1)}, bf16[16,16,1280]{2,1,0:T(8,128)(2,1)}) custom-call(bf16[64,192,119]{2,1,0:T(8,128)(2,1)} %bitcast.16, s32[64,119]{1,0:T(8,128)} %mask_ref.1, bf16[64,192,119]{2,1,0:T(8,128)(2,1)} %bitcast.17, bf16[16,16,1280]{2,1,0:T(8,128)(2,1)} %gather.1.full_ref), custom_call_target="tpu_custom_call" | custom-call | tf_op jit(solution)/shard_map/layer/pallas_call | solution.py:256
  159.7 18.6 %reduce.1.grad_ref = f32[16,1280]{1,0:T(8,128)} custom-call(bf16[16,16,1280]{2,1,0:T(8,128)(2,1)} %get-tuple-element.31.part_ref), custom_call_target="tpu_custom_call" | custom-call | tf_op jit(solution)/shard_map/reduce/pallas_call | solution.py:397
  178.3 2.0 %update.1 = (f32[12,4,192]{2,1,0:T(4,128)}, f32[12,4,192]{2,1,0:T(4,128)}, f32[12,4,192]{2,1,0:T(4,128)}, f32[12,512]{1,0:T(8,128)}, f32[12,512]{1,0:T(8,128)}, ...) custom-call(f32[16,1280]{1,0:T(8,128)} %reduce.1.grad_ref, ...), custom_call_target="tpu_custom_call" | custom-call | tf_op jit(solution)/shard_map/update/pallas_call | solution.py:437

commit v3 on v2

--- a/solution.py
+++ b/solution.py
@@ -10,7 +10,9 @@
 FH = 256
 STEP = 10
 LANES = 128
-GROUP = 2
+FORWARD = (0, 1, 7, 8, 9, 12)
+BACKWARD = (0, 1, 5, 6, 9)
+GROUP = 16
 F32 = jnp.float32
 BF16 = jnp.bfloat16
 NN = (((1,), (0,)), ((), ()))
@@ -28,6 +30,7 @@
     big, w2f, vec_s, wqkv_ref, wo_ref, w1_ref, w2_ref,
     wqkvt, wot, w1t, w2t, cols, n1a, n2a, oa, ha, e_s,
     gqkv_ref, go_ref, g1_ref, g2_ref, ln_acc, pack_s,
+    q_s, k_s, v_s, d_s, c_s, dqkv_s, o_s, inv_s,
 ):
     step = pl.program_id(0)
     length = x_ref.shape[2]
@@ -115,54 +118,62 @@
     n1a[:width, :] = (xhat1 * gain1 + bias1).astype(BF16)
     qkv = mm(wqkvt[...], n1a[...])
 
-    sub = lax.broadcasted_iota(jnp.int32, (8, LANES), 0)
-    lane = lax.broadcasted_iota(jnp.int32, (8, LANES), 1)
-    tile_q = jnp.where(sub == 0, 1.0, 0.0)
-    tile_v = jnp.where(sub < 2, 1.0, 0.0)
-    zeros = jnp.zeros((32, LANES), BF16)
-
-    def padded(rows, tail):
-        return jnp.concatenate([rows, tail], axis=0).astype(BF16)
-
-    def pair_diag(a, b):
-        return jnp.concatenate(
-            [jnp.concatenate([a, zeros], axis=1), jnp.concatenate([zeros, b], axis=1)], axis=0
-        )
-
-    kept = []
-    mixed = []
-    for g in range(group):
+    sub = lax.broadcasted_iota(jnp.int32, (16, LANES), 0)
+    lane = lax.broadcasted_iota(jnp.int32, (16, LANES), 1)
+    ones_q = jnp.where(sub == 0, 1.0, 0.0)
+    ones_v = jnp.where(sub < 2, 1.0, 0.0)
+    empty = jnp.zeros((head, LANES), F32)
+    two = 2 * head
+    live = {}
+
+    def block_diag(first, second, tail_first, tail_second):
+        left = jnp.concatenate([first, empty, tail_first], axis=0).astype(BF16)
+        right = jnp.concatenate([empty, second, tail_second], axis=0).astype(BF16)
+        return jnp.concatenate([left, right], axis=1)
+
+    def run(stages, lags):
+        items = [(g, p) for g in range(group) for p in range(H // 2)]
+        for t in range(len(items) + max(lags)):
+            for stage, lag in reversed(list(zip(stages, lags))):
+                if 0 <= t - lag < len(items):
+                    stage(t - lag, *items[t - lag])
+
+    def forward_prepare(t, g, p):
         sl = slice(g * LANES, (g + 1) * LANES)
         m = mask_ref[pl.ds(step * group + g, 1), :]
         m = jnp.concatenate([m, jnp.zeros((1, LANES - length), jnp.int32)], axis=1)
-        m8 = jnp.broadcast_to(m, (8, LANES))
-        ok = (m8 != 0) | (lane == 0)
-        tile_k = jnp.where((sub == 0) & jnp.logical_not(ok), -1e30, 0.0)
-        mixed_rows = []
-        for p in range(H // 2):
-            qs, ks, vs = [], [], []
-            for h in (2 * p, 2 * p + 1):
-                r = slice(h * head, (h + 1) * head)
-                qs.append(padded(qkv[r.start : r.stop, sl], tile_q))
-                ks.append(padded(qkv[width + r.start : width + r.stop, sl], tile_k))
-                vs.append(padded(qkv[2 * width + r.start : 2 * width + r.stop, sl], tile_v))
-            qd = pair_diag(*qs)
-            kp = jnp.concatenate(ks, axis=0)
-            vp = jnp.concatenate(vs, axis=0)
-            s = mm(kp.T, qd)
-            top = jnp.max(s, 0, keepdims=True)
-            e = jnp.exp2((s - top) * (factor * log2e)).astype(BF16)
-            e_s[g, p] = e
-            num = mm(vp, e)
-            for j in range(2):
-                part = num[32 * j : 32 * j + 32, j * LANES : (j + 1) * LANES]
-                inv = 1.0 / part[head : head + 1]
-                o = part[:head] * inv
-                mixed_rows.append(o)
-                kept.append((inv, o))
-            kept[-1] = kept[-1] + (qd, kp, vp)
-        mixed.append(jnp.concatenate(mixed_rows, axis=0))
-    oa[:width, :] = jnp.concatenate(mixed, axis=1).astype(BF16)
+        ok = (jnp.broadcast_to(m, (16, LANES)) != 0) | (lane == 0)
+        tail_k = jnp.where((sub == 0) & jnp.logical_not(ok), -1e30, 0.0)
+        lo = p * two
+        q_s[g, p] = block_diag(qkv[lo : lo + head, sl], qkv[lo + head : lo + two, sl], ones_q, ones_q)
+        kp = jnp.concatenate([qkv[width + lo : width + lo + two, sl], tail_k], axis=0).astype(BF16)
+        k_s[g, p] = kp
+        v_s[g, p] = jnp.concatenate([qkv[2 * width + lo : 2 * width + lo + two, sl], ones_v], axis=0).astype(BF16)
+        live["k", t] = kp.T
+
+    def forward_scores(t, g, p):
+        live["s", t] = mm(live.pop(("k", t)), q_s[g, p])
+
+    def forward_top(t, g, p):
+        live["m", t] = jnp.max(live["s", t], 0, keepdims=True)
+
+    def forward_exp(t, g, p):
+        e_s[g, p] = jnp.exp2((live.pop(("s", t)) - live.pop(("m", t))) * (factor * log2e)).astype(BF16)
+
+    def forward_mix(t, g, p):
+        live["n", t] = mm(v_s[g, p], e_s[g, p])
+
+    def forward_out(t, g, p):
+        num = live.pop(("n", t))
+        inv = 1.0 / num[two : two + 1]
+        inv_s[g, p : p + 1, :] = inv
+        sl = slice(g * LANES, (g + 1) * LANES)
+        lo = p * two
+        o_s[lo : lo + head, sl] = num[:head, :LANES] * inv[:, :LANES]
+        o_s[lo + head : lo + two, sl] = num[head:two, LANES:] * inv[:, LANES:]
+
+    run([forward_prepare, forward_scores, forward_top, forward_exp, forward_mix, forward_out], FORWARD)
+    oa[:width, :] = o_s[...].astype(BF16)
     x1 = x + mm(wot[...], oa[...])
     xhat2, rstd2 = norm(x1)
     n2a[:width, :] = (xhat2 * gain2 + bias2).astype(BF16)
@@ -188,35 +199,42 @@
     go_ref[...] += mm(oa[:208, :], da1, NT)
     do = mm(wo_ref[...], da1).astype(BF16).astype(F32)
 
-    parts = []
-    for g in range(group):
+    def backward_prepare(t, g, p):
         sl = slice(g * LANES, (g + 1) * LANES)
-        dqs, dks, dvs = [], [], []
-        for p in range(H // 2):
-            ds_ = []
-            for j in range(2):
-                h = 2 * p + j
-                inv, o = kept[g * H + h][:2]
-                d = do[h * head : (h + 1) * head, sl]
-                low = jnp.sum(d * o, 0, keepdims=True) * -inv
-                hi = low.astype(BF16).astype(F32)
-                lo = low - hi
-                tail = jnp.where(sub == 0, hi, jnp.where(sub == 1, lo, 0.0))
-                ds_.append(padded(d * inv, tail))
-            qd, kp, vp = kept[g * H + 2 * p + 1][2:]
-            dd = pair_diag(*ds_)
-            e = e_s[g, p]
-            dpd = mm(vp.T, dd)
-            dsc = (e.astype(F32) * dpd).astype(BF16)
-            dv = mm(dd, e, NT)
-            dq = mm(kp, dsc)
-            dk = mm(qd, dsc, NT)
-            for j in range(2):
-                dqs.append(dq[32 * j : 32 * j + head, j * LANES : (j + 1) * LANES] * factor)
-                dks.append(dk[32 * j : 32 * j + head] * factor)
-                dvs.append(dv[32 * j : 32 * j + head])
-        parts.append(jnp.concatenate(dqs + dks + dvs, axis=0))
-    dqkv = jnp.concatenate(parts, axis=1).astype(BF16)
+        rows, tails = [], []
+        for j in range(2):
+            r = slice(p * two + j * head, p * two + (j + 1) * head)
+            d = do[r, sl]
+            inv = inv_s[g, p : p + 1, j * LANES : (j + 1) * LANES]
+            low = jnp.sum(d * o_s[r, sl], 0, keepdims=True) * -inv
+            hi = low.astype(BF16).astype(F32)
+            rows.append(d * inv)
+            tails.append(jnp.where(sub == 0, hi, jnp.where(sub == 1, low - hi, 0.0)))
+        d_s[g, p] = block_diag(*rows, *tails)
+        live["v", t] = v_s[g, p].T
+
+    def backward_probs(t, g, p):
+        live["p", t] = mm(live.pop(("v", t)), d_s[g, p])
+
+    def backward_scores(t, g, p):
+        c_s[g, p] = (e_s[g, p].astype(F32) * live.pop(("p", t))).astype(BF16)
+
+    def backward_mix(t, g, p):
+        live["dv", t] = mm(d_s[g, p, :two], e_s[g, p], NT)
+        live["dk", t] = mm(q_s[g, p, :two], c_s[g, p], NT)
+        live["dq", t] = mm(k_s[g, p, :two], c_s[g, p])
+
+    def backward_out(t, g, p):
+        sl = slice(g * LANES, (g + 1) * LANES)
+        lo = p * two
+        dq = live.pop(("dq", t))
+        dq = jnp.concatenate([dq[:head, :LANES], dq[head:, LANES:]], axis=0)
+        dqkv_s[lo : lo + two, sl] = (dq * factor).astype(BF16)
+        dqkv_s[width + lo : width + lo + two, sl] = (live.pop(("dk", t)) * factor).astype(BF16)
+        dqkv_s[2 * width + lo : 2 * width + lo + two, sl] = live.pop(("dv", t)).astype(BF16)
+
+    run([backward_prepare, backward_probs, backward_scores, backward_mix, backward_out], BACKWARD)
+    dqkv = dqkv_s[...]
     gqkv_ref[...] += mm(n1a[:208, :], dqkv, NT)
     dn1 = mm(wqkv_ref[...], dqkv)
     dx = (dx1 + norm_back(dn1, xhat1, rstd1, gain1, 0)).astype(BF16)
@@ -283,6 +301,14 @@
             pltpu.VMEM((272, width), F32),
             pltpu.VMEM((4, width, LANES), F32),
             pltpu.VMEM(full.shape, F32),
+            pltpu.VMEM((group, H // 2, 64, 2 * LANES), BF16),
+            pltpu.VMEM((group, H // 2, 64, LANES), BF16),
+            pltpu.VMEM((group, H // 2, 64, LANES), BF16),
+            pltpu.VMEM((group, H // 2, 64, 2 * LANES), BF16),
+            pltpu.VMEM((group, H // 2, LANES, 2 * LANES), BF16),
+            pltpu.VMEM((3 * width, tokens), BF16),
+            pltpu.VMEM((width, tokens), F32),
+            pltpu.VMEM((group, H // 2, 2 * LANES), F32),
         ],
         compiler_params=pltpu.CompilerParams(vmem_limit_bytes=60 * 1024 * 1024),
         name="layer",

time: 181 us -> 91.1 us (0.50)
  Pallas kernels: 180 us -> 90 us
    pallas_call x1, Pallas kernels: 144 us -> 54.3 us  [run_layer(): pl.pallas_call(functools.partial(layer_kernel, group), grid=(samples // g...]
where the time goes in v3:
time: 91.1 us; the launch traced here: 90.7 us
  Pallas kernels  90 us (99%)
    pallas_call x1, Pallas kernels, run_layer(): pl.pallas_call(functools.partial(layer_kernel, group), grid=(samples // g...  54.3 us
    pallas_call x1, Pallas kernels, reduce_shares(): pl.pallas_call(functools.partial(reduce_kernel, n, copies_of), out_shape=...  18.6 us
    pallas_call x1, Pallas kernels, gather(): pl.pallas_call(functools.partial(gather_kernel, n), out_shape=jax.ShapeDt...  15.1 us
    pallas_call x1, Pallas kernels, update(): pl.pallas_call(update_kernel, out_shape=[jax.ShapeDtypeStruct(a.shape, F3...  2.04 us

profile of v3, /device:TPU:0, one launch (start us, length us, event | category | flops | bytes accessed | tf_op | source)
XLA Modules:
  0.0 90.7 jit_solution(7883521960190579154)
XLA Ops:
  0.6 15.1 %gather.1.full_ref = bf16[16,16,1280]{2,1,0:T(8,128)(2,1)} custom-call(f32[12,4,192]{2,1,0:T(4,128)} %bitcast.18, f32[12,512]{1,0:T(8,128)} %refs_3_.1, f32[16,192]{1,0:T(8,128)} %refs_6_.1, f32[1,128]{1,0:T(1,128)} %bitcast.22), custom_call_target="tpu_custom_call" | custom-call | tf_op jit(solution)/shard_map/gather/pallas_call | solution.py:369
  15.8 54.3 %layer.1 = (bf16[64,192,119]{2,1,0:T(8,128)(2,1)}, bf16[64,192,119]{2,1,0:T(8,128)(2,1)}, bf16[16,16,1280]{2,1,0:T(8,128)(2,1)}) custom-call(bf16[64,192,119]{2,1,0:T(8,128)(2,1)} %bitcast.16, s32[64,119]{1,0:T(8,128)} %mask_ref.1, bf16[64,192,119]{2,1,0:T(8,128)(2,1)} %bitcast.17, bf16[16,16,1280]{2,1,0:T(8,128)(2,1)} %gather.1.full_ref), custom_call_target="tpu_custom_call" | custom-call | tf_op jit(solution)/shard_map/layer/pallas_call | solution.py:274
  70.1 18.6 %reduce.1.grad_ref = f32[16,1280]{1,0:T(8,128)} custom-call(bf16[16,16,1280]{2,1,0:T(8,128)(2,1)} %get-tuple-element.31.part_ref), custom_call_target="tpu_custom_call" | custom-call | tf_op jit(solution)/shard_map/reduce/pallas_call | solution.py:423
  88.7 2.0 %update.1 = (f32[12,4,192]{2,1,0:T(4,128)}, f32[12,4,192]{2,1,0:T(4,128)}, f32[12,4,192]{2,1,0:T(4,128)}, f32[12,512]{1,0:T(8,128)}, f32[12,512]{1,0:T(8,128)}, ...) custom-call(f32[16,1280]{1,0:T(8,128)} %reduce.1.grad_ref, ...), custom_call_target="tpu_custom_call" | custom-call | tf_op jit(solution)/shard_map/update/pallas_call | solution.py:463

commit v4 on v3

--- a/solution.py
+++ b/solution.py
@@ -11,7 +11,7 @@
 STEP = 10
 LANES = 128
 FORWARD = (0, 1, 7, 8, 9, 12)
-BACKWARD = (0, 1, 5, 6, 9)
+BACKWARD = (0, 1, 1, 5, 6, 9)
 GROUP = 16
 F32 = jnp.float32
 BF16 = jnp.bfloat16
@@ -29,8 +29,8 @@
     y_ref, dx_ref, packed_ref,
     big, w2f, vec_s, wqkv_ref, wo_ref, w1_ref, w2_ref,
     wqkvt, wot, w1t, w2t, cols, n1a, n2a, oa, ha, e_s,
-    gqkv_ref, go_ref, g1_ref, g2_ref, ln_acc, pack_s,
-    q_s, k_s, v_s, d_s, c_s, dqkv_s, o_s, inv_s,
+    gqkv_ref, go_ref, g1_ref, g2_ref, ln_acc, pack_s, gqkvt_ref,
+    q_s, k_s, v_s, d_s, c_s, dqkv_s, o_s, inv_s, et_s,
 ):
     step = pl.program_id(0)
     length = x_ref.shape[2]
@@ -42,12 +42,12 @@
 
     @pl.when(step == 0)
     def _():
-        shards, block_rows, _ = full_ref.shape
+        shards, _, block_rows, _ = full_ref.shape
         depth = width // shards
         extra = block_rows - depth
         per_vec = vec_s.shape[1] // shards
         for w in range(shards):
-            block = full_ref[w].astype(F32)
+            block = jnp.concatenate([full_ref[w, 0], full_ref[w, 1]], axis=1).astype(F32)
             big[w * depth : (w + 1) * depth, :] = block[:depth]
             for j in range(4):
                 at = (4 * w + j) * extra
@@ -79,7 +79,7 @@
         n2a[width:, :] = one
         oa[width:, :] = one
         ha[FH:, :] = one[:16]
-        gqkv_ref[...] = jnp.zeros_like(gqkv_ref)
+        gqkvt_ref[...] = jnp.zeros_like(gqkvt_ref)
         go_ref[...] = jnp.zeros_like(go_ref)
         g1_ref[...] = jnp.zeros_like(g1_ref)
         g2_ref[...] = jnp.zeros_like(g2_ref)
@@ -212,6 +212,7 @@
             tails.append(jnp.where(sub == 0, hi, jnp.where(sub == 1, low - hi, 0.0)))
         d_s[g, p] = block_diag(*rows, *tails)
         live["v", t] = v_s[g, p].T
+        live["r", t] = jnp.concatenate(rows, axis=0).astype(BF16)
 
     def backward_probs(t, g, p):
         live["p", t] = mm(live.pop(("v", t)), d_s[g, p])
@@ -219,8 +220,12 @@
     def backward_scores(t, g, p):
         c_s[g, p] = (e_s[g, p].astype(F32) * live.pop(("p", t))).astype(BF16)
 
+    def backward_turn(t, g, p):
+        e = e_s[g, p]
+        et_s[g, p] = jnp.concatenate([e[:, :LANES].T, e[:, LANES:].T], axis=1)
+
     def backward_mix(t, g, p):
-        live["dv", t] = mm(d_s[g, p, :two], e_s[g, p], NT)
+        live["dv", t] = mm(live.pop(("r", t)), et_s[g, p])
         live["dk", t] = mm(q_s[g, p, :two], c_s[g, p], NT)
         live["dq", t] = mm(k_s[g, p, :two], c_s[g, p])
 
@@ -231,11 +236,13 @@
         dq = jnp.concatenate([dq[:head, :LANES], dq[head:, LANES:]], axis=0)
         dqkv_s[lo : lo + two, sl] = (dq * factor).astype(BF16)
         dqkv_s[width + lo : width + lo + two, sl] = (live.pop(("dk", t)) * factor).astype(BF16)
-        dqkv_s[2 * width + lo : 2 * width + lo + two, sl] = live.pop(("dv", t)).astype(BF16)
-
-    run([backward_prepare, backward_probs, backward_scores, backward_mix, backward_out], BACKWARD)
+        dv = live.pop(("dv", t))
+        dv = jnp.concatenate([dv[:head, :LANES], dv[head:, LANES:]], axis=0)
+        dqkv_s[2 * width + lo : 2 * width + lo + two, sl] = dv.astype(BF16)
+
+    run([backward_prepare, backward_turn, backward_probs, backward_scores, backward_mix, backward_out], BACKWARD)
     dqkv = dqkv_s[...]
-    gqkv_ref[...] += mm(n1a[:208, :], dqkv, NT)
+    gqkvt_ref[...] += mm(dqkv, n1a[:208, :], NT)
     dn1 = mm(wqkv_ref[...], dqkv)
     dx = (dx1 + norm_back(dn1, xhat1, rstd1, gain1, 0)).astype(BF16)
     for g in range(group):
@@ -243,13 +250,14 @@
 
     @pl.when(step == pl.num_programs(0) - 1)
     def _():
+        gqkv_ref[...] = gqkvt_ref[...].T
         rows = [jnp.sum(ln_acc[i].T, 0, keepdims=True) for i in range(4)]
         vec = jnp.concatenate(
             [rows[0], rows[1], gqkv_ref[width : width + 1, :width], gqkv_ref[width : width + 1, 2 * width :],
              go_ref[width : width + 1], rows[2], rows[3], g2_ref[FH : FH + 1], g1_ref[width : width + 1]],
             axis=1,
         )
-        shards, block_rows, _ = packed_ref.shape
+        shards, _, block_rows, half = packed_ref.shape
         depth = width // shards
         extra = block_rows - depth
         per_vec = vec.shape[1] // shards
@@ -263,7 +271,8 @@
                 [g2_ref[at + j * extra : at + (j + 1) * extra, :] for j in range(4)], axis=1
             )
             pack_s[w, depth : depth + 1, 4 * width : 4 * width + per_vec] = vec[:, w * per_vec : (w + 1) * per_vec]
-        packed_ref[...] = pack_s[...].astype(BF16)
+        for j in range(2):
+            packed_ref[:, j] = pack_s[:, :, j * half : (j + 1) * half].astype(BF16)
 
 
 def run_layer(x, mask, dout, full, group):
@@ -300,7 +309,8 @@
             pltpu.VMEM((208, 2 * FH), F32),
             pltpu.VMEM((272, width), F32),
             pltpu.VMEM((4, width, LANES), F32),
-            pltpu.VMEM(full.shape, F32),
+            pltpu.VMEM((full.shape[0], full.shape[2], 2 * full.shape[3]), F32),
+            pltpu.VMEM((3 * width, 208), F32),
             pltpu.VMEM((group, H // 2, 64, 2 * LANES), BF16),
             pltpu.VMEM((group, H // 2, 64, LANES), BF16),
             pltpu.VMEM((group, H // 2, 64, LANES), BF16),
@@ -309,6 +319,7 @@
             pltpu.VMEM((3 * width, tokens), BF16),
             pltpu.VMEM((width, tokens), F32),
             pltpu.VMEM((group, H // 2, 2 * LANES), F32),
+            pltpu.VMEM((group, H // 2, LANES, 2 * LANES), BF16),
         ],
         compiler_params=pltpu.CompilerParams(vmem_limit_bytes=60 * 1024 * 1024),
         name="layer",
@@ -324,109 +335,142 @@
     return copy
 
 
-def meet(devices):
+def hail(devices):
     barrier = pltpu.get_barrier_semaphore()
     for device in devices:
         pl.semaphore_signal(barrier, inc=1, device_id=device, device_id_type=pl.DeviceIdType.MESH)
-    pl.semaphore_wait(barrier, len(devices))
-
-
-def gather_kernel(n, attn_ref, w1_ref, w2_ref, vec_ref, out_ref, send1, recv1, send2, recv2):
-    me = lax.axis_index("wide")
+
+
+def places(n, copies_of):
+    me, mine = lax.axis_index("wide"), lax.axis_index("narrow")
     core, chip, chips = lax.rem(me, 2), lax.div(me, 2), n // 2
-    peer = lambda k: 2 * lax.rem(chip + k, chips) + core
+    peer = lambda k: 2 * lax.bitwise_xor(chip, k) + core
+    half = lax.rem(mine, 2)
     sibling = {"wide": me + 1 - 2 * core}
-    depth = attn_ref.shape[0]
+    twin = {"narrow": mine + 1 - 2 * half}
+    return me, mine, core, chips, peer, half, sibling, twin
+
+
+def gather_kernel(n, copies_of, attn_hbm, w1_hbm, w2_hbm, vec_hbm, out_ref, attn_ref, w1_ref, w2_ref, vec_ref, load,
+                  send1, recv1, send2, recv2, send3, recv3, send4, recv4):
+    me, mine, core, chips, peer, half, sibling, twin = places(n, copies_of)
+    met = [{"wide": peer(k)} for k in range(1, chips)] + [sibling, twin]
+    hail(met)
+    pairs = ((attn_hbm, attn_ref), (w1_hbm, w1_ref), (w2_hbm, w2_ref), (vec_hbm, vec_ref))
+    loads = [pltpu.make_async_copy(a, b, load.at[i]) for i, (a, b) in enumerate(pairs)]
+    for copy in loads:
+        copy.start()
+    for copy in loads:
+        copy.wait()
     width = attn_ref.shape[2]
     extra = w2_ref.shape[0] // 4
-    lanes = out_ref.shape[2]
+    lanes = out_ref.shape[3]
     top = jnp.concatenate([attn_ref[:, i, :] for i in range(4)] + [w1_ref[...]], axis=1)
     bottom = jnp.concatenate(
         [w2_ref[j * extra : (j + 1) * extra, :] for j in range(4)]
         + [jnp.broadcast_to(vec_ref[...], (extra, vec_ref.shape[1])),
-           jnp.zeros((extra, lanes - 4 * width - vec_ref.shape[1]), F32)],
+           jnp.zeros((extra, 2 * lanes - 4 * width - vec_ref.shape[1]), F32)],
         axis=1,
     )
-    out_ref[me] = jnp.concatenate([top, bottom], axis=0).astype(BF16)
-    meet([{"wide": peer(k)} for k in range(1, chips)] + [sibling])
-    mine = out_ref.at[me]
-    copies = [send(mine, mine, send1.at[k], recv1.at[k], {"wide": peer(k)}) for k in range(1, chips)]
-    passed = [send(mine, mine, send2.at[0], recv2.at[0], sibling)]
+    block = jnp.concatenate([top, bottom], axis=0).astype(BF16)
+    out_ref[me, 0] = block[:, :lanes]
+    out_ref[me, 1] = block[:, lanes:]
+    pl.semaphore_wait(pltpu.get_barrier_semaphore(), len(met))
+    own = out_ref.at[me, half]
+    copies = {}
+    for k in reversed(range(1, chips)):
+        copies[k] = send(own, own, send1.at[k], recv1.at[k], {"wide": peer(k)})
+    whole = out_ref.at[me]
+    passed = [send(whole, whole, send2.at[0], recv2.at[0], sibling)]
+    crossed = {}
     for k in range(1, chips):
-        copies[k - 1].wait_recv()
-        block = out_ref.at[peer(chips - k)]
-        passed.append(send(block, block, send2.at[k], recv2.at[k], sibling))
-    for copy in copies:
+        copies[k].wait_recv()
+        got = out_ref.at[peer(k), half]
+        crossed[k] = send(got, got, send3.at[k], recv3.at[k], twin)
+        passed.append(send(got, got, send2.at[k], recv2.at[k], sibling))
+    for k in range(1, chips):
+        crossed[k].wait_recv()
+        got = out_ref.at[peer(k), 1 - half]
+        passed.append(send(got, got, send4.at[k], recv4.at[k], sibling))
+    for copy in list(copies.values()) + list(crossed.values()):
         copy.wait_send()
     for copy in passed:
         copy.wait()
 
 
-def gather(attn, w1, w2, vec, n):
+def gather(attn, w1, w2, vec, n, copies_of):
     rows = attn.shape[0] + w2.shape[0] // 4
     lanes = 4 * attn.shape[2] + w1.shape[1]
     sems = pltpu.SemaphoreType.DMA((n // 2,))
     return pl.pallas_call(
-        functools.partial(gather_kernel, n),
-        out_shape=jax.ShapeDtypeStruct((n, rows, lanes), BF16),
-        in_specs=[pl.BlockSpec(memory_space=pltpu.VMEM)] * 4,
+        functools.partial(gather_kernel, n, copies_of),
+        out_shape=jax.ShapeDtypeStruct((n, 2, rows, lanes // 2), BF16),
+        in_specs=[pl.BlockSpec(memory_space=pl.ANY)] * 4,
         out_specs=pl.BlockSpec(memory_space=pltpu.VMEM),
-        scratch_shapes=[sems] * 4,
+        scratch_shapes=[pltpu.VMEM(a.shape, F32) for a in (attn, w1, w2, vec)]
+        + [pltpu.SemaphoreType.DMA((4,))] + [sems] * 8,
         compiler_params=pltpu.CompilerParams(collective_id=0, has_side_effects=True),
         name="gather",
     )(attn, w1, w2, vec)
 
 
-def reduce_kernel(n, copies_of, part_ref, out_ref, core_buf, sum_buf, wide_buf, narrow_buf,
-                  send0, recv0, send1, recv1, send2, recv2):
-    me, mine = lax.axis_index("wide"), lax.axis_index("narrow")
-    core, chip, chips = lax.rem(me, 2), lax.div(me, 2), n // 2
-    peer = lambda k: 2 * lax.rem(chip + k, chips) + core
-    sibling = {"wide": me + 1 - 2 * core}
-    twin = lambda j: {"narrow": lax.rem(mine + j, copies_of)}
-    meet([{"wide": peer(k)} for k in range(1, chips)] + [sibling] + [twin(j) for j in range(1, copies_of)])
-    order = list(range(1, chips)) + [0]
-    first = {}
+def reduce_kernel(n, copies_of, part_hbm, out_ref, part_ref, core_buf, keep_buf, turn_buf, twin_buf, sum_buf,
+                  wide_buf, narrow_buf, load, send0, recv0, send1, recv1, send2, recv2, send3, recv3):
+    me, mine, core, chips, peer, half, sibling, twin = places(n, copies_of)
+    others = [{"narrow": lax.rem(mine + j, copies_of)} for j in range(1, copies_of)]
+    met = [{"wide": peer(k)} for k in range(1, chips)] + [sibling] + others
+    hail(met)
+    mine_parts = pltpu.make_async_copy(part_hbm, part_ref, load)
+    mine_parts.start()
+    mine_parts.wait()
+    pl.semaphore_wait(pltpu.get_barrier_semaphore(), len(met))
+    order = list(reversed(range(chips)))
+    first, second, third = {}, {}, {}
     for k in order:
-        other = peer(k) + 1 - 2 * core
-        first[k] = send(part_ref.at[other], core_buf.at[k], send0.at[k], recv0.at[k], sibling)
-    second = {}
+        first[k] = send(part_ref.at[peer(k) + 1 - 2 * core], core_buf.at[k], send0.at[k], recv0.at[k], sibling)
     for k in order:
         first[k].wait_recv()
-        total = part_ref[peer(k)].astype(F32) + core_buf[k].astype(F32)
+        turn_buf[k] = (part_ref[peer(k), 1 - half].astype(F32) + core_buf[k, 1 - half].astype(F32)).astype(BF16)
+        second[k] = send(turn_buf.at[k], twin_buf.at[k], send1.at[k], recv1.at[k], twin)
+        keep_buf[k] = part_ref[peer(k), half].astype(F32) + core_buf[k, half].astype(F32)
+    for k in order:
+        second[k].wait_recv()
+        total = keep_buf[k] + twin_buf[k].astype(F32)
         if k:
             sum_buf[k] = total.astype(BF16)
-            second[k] = send(sum_buf.at[k], wide_buf.at[k], send1.at[k], recv1.at[k], {"wide": peer(k)})
+            third[k] = send(sum_buf.at[k], wide_buf.at[k], send2.at[k], recv2.at[k], {"wide": peer(k)})
     for k in range(1, chips):
-        second[k].wait_recv()
+        third[k].wait_recv()
         total = total + wide_buf[k].astype(F32)
     narrow_buf[mine] = total
-    third = [
-        send(narrow_buf.at[mine], narrow_buf.at[mine], send2.at[j], recv2.at[j], twin(j))
-        for j in range(1, copies_of)
-    ]
-    for copy in third:
+    slot = narrow_buf.at[mine]
+    fourth = [send(slot, slot, send3.at[j], recv3.at[j], other) for j, other in enumerate(others)]
+    for copy in fourth:
         copy.wait_recv()
-    result = narrow_buf[0]
-    for j in range(1, copies_of):
-        result = result + narrow_buf[j]
-    out_ref[...] = result
-    for copy in list(first.values()) + list(second.values()) + third:
+    lanes = total.shape[1]
+    for h in range(2):
+        result = narrow_buf[h]
+        for j in range(h + 2, copies_of, 2):
+            result = result + narrow_buf[j]
+        out_ref[:, h * lanes : (h + 1) * lanes] = result
+    for copy in list(first.values()) + list(second.values()) + list(third.values()) + fourth:
         copy.wait_send()
 
 
 def reduce_shares(packed, n, copies_of):
     chips = n // 2
-    block = packed.shape[1:]
+    rows, lanes = packed.shape[2:]
     sems = pltpu.SemaphoreType.DMA((chips,))
     few = pltpu.SemaphoreType.DMA((copies_of,))
+    part = lambda kind: pltpu.VMEM((chips, rows, lanes), kind)
     return pl.pallas_call(
         functools.partial(reduce_kernel, n, copies_of),
-        out_shape=jax.ShapeDtypeStruct(block, F32),
-        in_specs=[pl.BlockSpec(memory_space=pltpu.VMEM)],
+        out_shape=jax.ShapeDtypeStruct((rows, 2 * lanes), F32),
+        in_specs=[pl.BlockSpec(memory_space=pl.ANY)],
         out_specs=pl.BlockSpec(memory_space=pltpu.VMEM),
-        scratch_shapes=[pltpu.VMEM((chips,) + block, BF16)] * 3
-        + [pltpu.VMEM((copies_of,) + block, F32), sems, sems, sems, sems, few, few],
+        scratch_shapes=[pltpu.VMEM(packed.shape, BF16), pltpu.VMEM((chips, 2, rows, lanes), BF16), part(F32),
+                        part(BF16), part(BF16), part(BF16), part(BF16), pltpu.VMEM((copies_of, rows, lanes), F32),
+                        pltpu.SemaphoreType.DMA] + [sems] * 6 + [few] * 2,
         compiler_params=pltpu.CompilerParams(collective_id=1, has_side_effects=True),
         name="reduce",
     )(packed)
@@ -474,7 +518,7 @@
     n, copies_of = lax.axis_size("wide"), lax.axis_size("narrow")
     turn = lambda a: a.transpose(1, 0, 2)
     row = lambda a: a.reshape(1, -1)
-    full = gather(turn(attn_w), ffn_in, ffn_out, row(vec), n)
+    full = gather(turn(attn_w), ffn_in, ffn_out, row(vec), n, copies_of)
     y, dx, packed = run_layer(layer_input.transpose(0, 2, 1), mask, dout.transpose(0, 2, 1), full, GROUP)
     share = reduce_shares(packed, n, copies_of)
     new = update(share, [turn(attn_w), turn(m_attn), turn(v_attn), ffn_in, m_in, v_in, ffn_out, m_out, v_out,

time: 91.1 us -> 86.9 us (0.954)
  Pallas kernels: 90 us -> 86 us
    pallas_call x1, Pallas kernels: 54.3 us -> 50.9 us  [run_layer(): pl.pallas_call(functools.partial(layer_kernel, group), grid=(samples // g...]
    pallas_call x1, Pallas kernels: 18.6 us -> 16.3 us  [reduce_shares(): pl.pallas_call(functools.partial(reduce_kernel, n, copies_of), out_shape=...]
    pallas_call x1, Pallas kernels: 15.1 us -> 16.8 us  [gather(): pl.pallas_call(functools.partial(gather_kernel, n, copies_of), out_shape=...]
where the time goes in v4:
time: 86.9 us; the launch traced here: 86.6 us
  Pallas kernels  86 us (99%)
    pallas_call x1, Pallas kernels, run_layer(): pl.pallas_call(functools.partial(layer_kernel, group), grid=(samples // g...  50.9 us
    pallas_call x1, Pallas kernels, gather(): pl.pallas_call(functools.partial(gather_kernel, n, copies_of), out_shape=...  16.8 us
    pallas_call x1, Pallas kernels, reduce_shares(): pl.pallas_call(functools.partial(reduce_kernel, n, copies_of), out_shape=...  16.3 us
    pallas_call x1, Pallas kernels, update(): pl.pallas_call(update_kernel, out_shape=[jax.ShapeDtypeStruct(a.shape, F3...  2.04 us

profile of v4, /device:TPU:0, one launch (start us, length us, event | category | flops | bytes accessed | tf_op | source)
XLA Modules:
  0.0 86.6 jit_solution(9214534437112513452)
XLA Ops:
  0.6 16.8 %gather.1.full_ref = bf16[16,2,16,640]{3,2,1,0:T(8,128)(2,1)} custom-call(f32[12,4,192]{2,1,0:T(4,128)} %bitcast.18, f32[12,512]{1,0:T(8,128)} %refs_3_.1, f32[16,192]{1,0:T(8,128)} %refs_6_.1, f32[1,128]{1,0:T(1,128)} %bitcast.22), custom_call_target="tpu_custom_call" | custom-call | tf_op jit(solution)/shard_map/gather/pallas_call | solution.py:405
  17.4 50.9 %layer.1 = (bf16[64,192,119]{2,1,0:T(8,128)(2,1)}, bf16[64,192,119]{2,1,0:T(8,128)(2,1)}, bf16[16,2,16,640]{3,2,1,0:T(8,128)(2,1)}) custom-call(bf16[64,192,119]{2,1,0:T(8,128)(2,1)} %bitcast.16, s32[64,119]{1,0:T(8,128)} %mask_ref.1, bf16[64,192,119]{2,1,0:T(8,128)(2,1)} %bitcast.17, bf16[16,2,16,640]{3,2,1,0:T(8,128)(2,1)} %gather.1.full_ref), custom_call_target="tpu_custom_call" | custom-call | tf_op jit(solution)/shard_map/layer/pallas_call | solution.py:283
  68.3 16.3 %reduce.1.grad_ref = f32[16,1280]{1,0:T(8,128)} custom-call(bf16[16,2,16,640]{3,2,1,0:T(8,128)(2,1)} %get-tuple-element.31.part_hbm), custom_call_target="tpu_custom_call" | custom-call | tf_op jit(solution)/shard_map/reduce/pallas_call | solution.py:466
  84.6 2.0 %update.1 = (f32[12,4,192]{2,1,0:T(4,128)}, f32[12,4,192]{2,1,0:T(4,128)}, f32[12,4,192]{2,1,0:T(4,128)}, f32[12,512]{1,0:T(8,128)}, f32[12,512]{1,0:T(8,128)}, ...) custom-call(f32[16,1280]{1,0:T(8,128)} %reduce.1.grad_ref, ...), custom_call_target="tpu_custom_call" | custom-call | tf_op jit(solution)/shard_map/update/pallas_call | solution.py:507

commit v5 on v4

--- a/solution.py
+++ b/solution.py
@@ -29,7 +29,7 @@
     y_ref, dx_ref, packed_ref,
     big, w2f, vec_s, wqkv_ref, wo_ref, w1_ref, w2_ref,
     wqkvt, wot, w1t, w2t, cols, n1a, n2a, oa, ha, e_s,
-    gqkv_ref, go_ref, g1_ref, g2_ref, ln_acc, pack_s, gqkvt_ref,
+    gqkv_ref, go_ref, g1_ref, g2_ref, ln_acc, pack_s, gqkvt_ref, g1t_ref,
     q_s, k_s, v_s, d_s, c_s, dqkv_s, o_s, inv_s, et_s,
 ):
     step = pl.program_id(0)
@@ -81,7 +81,7 @@
         ha[FH:, :] = one[:16]
         gqkvt_ref[...] = jnp.zeros_like(gqkvt_ref)
         go_ref[...] = jnp.zeros_like(go_ref)
-        g1_ref[...] = jnp.zeros_like(g1_ref)
+        g1t_ref[...] = jnp.zeros_like(g1t_ref)
         g2_ref[...] = jnp.zeros_like(g2_ref)
         ln_acc[...] = jnp.zeros_like(ln_acc)
 
@@ -99,13 +99,10 @@
 
     def norm_back(dn, xhat, rstd, gain, which):
         prod = dn * xhat
-        a0, a1 = ln_acc[2 * which], ln_acc[2 * which + 1]
-        for g in range(group):
-            sl = slice(g * LANES, (g + 1) * LANES)
-            a0 = a0 + prod[:, sl]
-            a1 = a1 + dn[:, sl]
-        ln_acc[2 * which] = a0
-        ln_acc[2 * which + 1] = a1
+        total = ln_acc[which]
+        for g in range(dn.shape[1] // LANES):
+            total = total + prod[:, g * LANES : (g + 1) * LANES]
+        ln_acc[which] = total
         t = dn * gain
         m1 = jnp.sum(t, 0, keepdims=True) * (1.0 / width)
         m2 = jnp.sum(t * xhat, 0, keepdims=True) * (1.0 / width)
@@ -177,27 +174,33 @@
     x1 = x + mm(wot[...], oa[...])
     xhat2, rstd2 = norm(x1)
     n2a[:width, :] = (xhat2 * gain2 + bias2).astype(BF16)
-    z = mm(w1t[...], n2a[...])
-    part_a, part_b = z[:FH], z[FH:]
-    sigm = 1.0 / (1.0 + jnp.exp2(part_b * -log2e))
-    silu = part_b * sigm
-    ha[:FH, :] = (part_a * silu).astype(BF16)
-    y = (x1 + mm(w2t[...], ha[:FH, :]) + bias_c2).astype(BF16)
-    for g in range(group):
-        y_ref[g] = y[:, g * LANES : g * LANES + length]
-
     gt = jnp.concatenate([wide(g_ref, g) for g in range(group)], axis=1)
+    dz_tiles = []
+    for t in range(tokens // 256):
+        sl = slice(t * 256, (t + 1) * 256)
+        z = mm(w1t[...], n2a[:, sl])
+        dh = mm(w2_ref[...], gt[:, sl])
+        das, dbs = [], []
+        for c in range(FH // 64):
+            part_a, part_b = z[c * 64 : (c + 1) * 64], z[FH + c * 64 : FH + (c + 1) * 64]
+            grad = dh[c * 64 : (c + 1) * 64]
+            sigm = 1.0 / (1.0 + jnp.exp2(part_b * -log2e))
+            silu = part_b * sigm
+            ha[c * 64 : (c + 1) * 64, sl] = (part_a * silu).astype(BF16)
+            das.append((grad * silu).astype(BF16))
+            dbs.append((grad * part_a * (sigm + silu * (1.0 - sigm))).astype(BF16))
+        dz_tiles.append(jnp.concatenate(das + dbs, axis=0))
+    dz = jnp.concatenate(dz_tiles, axis=1)
     g2_ref[...] += mm(ha[...], gt, NT)
-    dh = mm(w2_ref[...], gt)
-    da = dh * silu
-    db = dh * part_a * sigm * (1.0 + part_b * (1.0 - sigm))
-    dz = jnp.concatenate([da, db], axis=0).astype(BF16)
-    g1_ref[...] += mm(n2a[:208, :], dz, NT)
+    g1t_ref[...] += mm(dz, n2a[:208, :], NT)
     dn2 = mm(w1_ref[...], dz)
     dx1 = gt.astype(F32) + norm_back(dn2, xhat2, rstd2, gain2, 1)
     da1 = dx1.astype(BF16)
     go_ref[...] += mm(oa[:208, :], da1, NT)
     do = mm(wo_ref[...], da1).astype(BF16).astype(F32)
+    y = (x1 + mm(w2t[...], ha[:FH, :]) + bias_c2).astype(BF16)
+    for g in range(group):
+        y_ref[g] = y[:, g * LANES : g * LANES + length]
 
     def backward_prepare(t, g, p):
         sl = slice(g * LANES, (g + 1) * LANES)
@@ -251,7 +254,13 @@
     @pl.when(step == pl.num_programs(0) - 1)
     def _():
         gqkv_ref[...] = gqkvt_ref[...].T
-        rows = [jnp.sum(ln_acc[i].T, 0, keepdims=True) for i in range(4)]
+        g1_ref[...] = g1t_ref[...].T
+        gains = [jnp.sum(ln_acc[i].T, 0, keepdims=True) for i in range(2)]
+
+        def through(weights, sums):
+            return jnp.sum(weights[:, :width].astype(F32) * sums[:, width : width + 1], 0, keepdims=True)
+
+        rows = [gains[0], through(wqkvt, gqkvt_ref), gains[1], through(w1t, g1t_ref)]
         vec = jnp.concatenate(
             [rows[0], rows[1], gqkv_ref[width : width + 1, :width], gqkv_ref[width : width + 1, 2 * width :],
              go_ref[width : width + 1], rows[2], rows[3], g2_ref[FH : FH + 1], g1_ref[width : width + 1]],
@@ -308,9 +317,10 @@
             pltpu.VMEM((208, width), F32),
             pltpu.VMEM((208, 2 * FH), F32),
             pltpu.VMEM((272, width), F32),
-            pltpu.VMEM((4, width, LANES), F32),
+            pltpu.VMEM((2, width, LANES), F32),
             pltpu.VMEM((full.shape[0], full.shape[2], 2 * full.shape[3]), F32),
             pltpu.VMEM((3 * width, 208), F32),
+            pltpu.VMEM((2 * FH, 208), F32),
             pltpu.VMEM((group, H // 2, 64, 2 * LANES), BF16),
             pltpu.VMEM((group, H // 2, 64, LANES), BF16),
             pltpu.VMEM((group, H // 2, 64, LANES), BF16),
@@ -471,7 +481,7 @@
         scratch_shapes=[pltpu.VMEM(packed.shape, BF16), pltpu.VMEM((chips, 2, rows, lanes), BF16), part(F32),
                         part(BF16), part(BF16), part(BF16), part(BF16), pltpu.VMEM((copies_of, rows, lanes), F32),
                         pltpu.SemaphoreType.DMA] + [sems] * 6 + [few] * 2,
-        compiler_params=pltpu.CompilerParams(collective_id=1, has_side_effects=True),
+        compiler_params=pltpu.CompilerParams(collective_id=1, has_side_effects=True, vmem_limit_bytes=56000000),
         name="reduce",
     )(packed)
 
@@ -509,6 +519,7 @@
         out_shape=[jax.ShapeDtypeStruct(a.shape, F32) for a in states],
         in_specs=[vmem] * 13,
         out_specs=[vmem] * 12,
+        compiler_params=pltpu.CompilerParams(vmem_limit_bytes=4 * 1024 * 1024),
         name="update",
     )(grad, *states)
 

time: 86.9 us -> 84.6 us (0.974)
  Pallas kernels: 86 us -> 83.5 us
    pallas_call x1, Pallas kernels: 2.04 us -> 1 us  [update(): pl.pallas_call(update_kernel, out_shape=[jax.ShapeDtypeStruct(a.shape, F3...]
where the time goes in v5:
time: 84.6 us; the launch traced here: 84.4 us
  Pallas kernels  83.5 us (99%)
  between operations  0.85 us (1%)
    pallas_call x1, Pallas kernels, run_layer(): pl.pallas_call(functools.partial(layer_kernel, group), grid=(samples // g...  50.1 us
    pallas_call x1, Pallas kernels, gather(): pl.pallas_call(functools.partial(gather_kernel, n, copies_of), out_shape=...  16.8 us
    pallas_call x1, Pallas kernels, reduce_shares(): pl.pallas_call(functools.partial(reduce_kernel, n, copies_of), out_shape=...  15.6 us

profile of v5, /device:TPU:0, one launch (start us, length us, event | category | flops | bytes accessed | tf_op | source)
XLA Modules:
  0.0 84.4 jit_solution(14749881082134861734)
XLA Ops:
  0.6 16.8 %gather.1.full_ref = bf16[16,2,16,640]{3,2,1,0:T(8,128)(2,1)} custom-call(f32[12,4,192]{2,1,0:T(4,128)} %bitcast.16, f32[12,512]{1,0:T(8,128)} %refs_3_.1, f32[16,192]{1,0:T(8,128)} %refs_6_.1, f32[1,128]{1,0:T(1,128)} %bitcast.20), custom_call_target="tpu_custom_call" | custom-call | tf_op jit(solution)/shard_map/gather/pallas_call | solution.py:415
  17.4 0.0 copy-start
  17.4 0.0 copy-start.1
  17.4 0.0 copy-start.2
  17.5 0.0 copy-start.3
  17.5 0.0 copy-start.4
  17.5 0.0 copy-start.5
  17.5 0.0 copy-start.6
  17.5 0.0 copy-start.7
  17.5 0.0 copy-start.8
  17.5 0.0 copy-start.9
  17.5 0.0 copy-start.10
  17.6 0.0 copy-start.11
  17.6 50.1 %layer.1 = (bf16[64,192,119]{2,1,0:T(8,128)(2,1)}, bf16[64,192,119]{2,1,0:T(8,128)(2,1)}, bf16[16,2,16,640]{3,2,1,0:T(8,128)(2,1)}) custom-call(bf16[64,192,119]{2,1,0:T(8,128)(2,1)} %bitcast.24, s32[64,119]{1,0:T(8,128)} %mask_ref.1, bf16[64,192,119]{2,1,0:T(8,128)(2,1)} %bitcast.25, bf16[16,2,16,640]{3,2,1,0:T(8,128)(2,1)} %gather.1.full_ref), custom_call_target="tpu_custom_call" | custom-call | tf_op jit(solution)/shard_map/layer/pallas_call | solution.py:292
  67.6 15.6 %reduce.1.grad_ref = f32[16,1280]{1,0:T(8,128)S(1)} custom-call(bf16[16,2,16,640]{3,2,1,0:T(8,128)(2,1)} %get-tuple-element.31.part_hbm), custom_call_target="tpu_custom_call" | custom-call | tf_op jit(solution)/shard_map/reduce/pallas_call | solution.py:476
  83.3 0.0 copy-done
  83.3 0.0 copy-done.1
  83.3 0.0 copy-done.2
  83.3 0.0 copy-done.3
  83.3 0.0 copy-done.4
  83.3 0.0 copy-done.5
  83.3 0.0 copy-done.6
  83.4 0.0 copy-done.7
  83.4 1.0 %update.1 = (f32[12,4,192]{2,1,0:T(4,128)}, f32[12,4,192]{2,1,0:T(4,128)}, f32[12,4,192]{2,1,0:T(4,128)}, f32[12,512]{1,0:T(8,128)}, f32[12,512]{1,0:T(8,128)}, ...) custom-call(f32[16,1280]{1,0:T(8,128)S(1)} %reduce.1.grad_ref, ...), custom_call_target="tpu_custom_call" | custom-call | tf_op jit(solution)/shard_map/update/pallas_call | solution.py:517
  (4 shorter events, 0.0 us)
Async XLA Ops:
  17.4 65.9 %copy-start = (f32[4,12,192]{2,0,1:T(4,128)S(1)}, f32[4,12,192]{2,0,1:T(4,128)}, u32[]{:S(2)}) copy-start(f32[4,12,192]{2,0,1:T(4,128)} %param.18) | copy-start | bytes 110596
  17.4 65.9 %copy-start.1 = (f32[12,512]{1,0:T(8,128)S(1)}, f32[12,512]{1,0:T(8,128)}, u32[]{:S(2)}) copy-start(f32[12,512]{1,0:T(8,128)} %refs_3_.1) | copy-start | bytes 73732
  17.4 65.9 %copy-start.2 = (f32[16,192]{1,0:T(8,128)S(1)}, f32[16,192]{1,0:T(8,128)}, u32[]{:S(2)}) copy-start(f32[16,192]{1,0:T(8,128)} %refs_6_.1) | copy-start | bytes 36868
  17.5 65.9 %copy-start.3 = (f32[4,12,192]{2,0,1:T(4,128)S(1)}, f32[4,12,192]{2,0,1:T(4,128)}, u32[]{:S(2)}) copy-start(f32[4,12,192]{2,0,1:T(4,128)} %param.22) | copy-start | bytes 110596
  17.5 65.9 %copy-start.4 = (f32[4,12,192]{2,0,1:T(4,128)S(1)}, f32[4,12,192]{2,0,1:T(4,128)}, u32[]{:S(2)}) copy-start(f32[4,12,192]{2,0,1:T(4,128)} %param.23) | copy-start | bytes 110596
  17.5 65.9 %copy-start.5 = (f32[12,512]{1,0:T(8,128)S(1)}, f32[12,512]{1,0:T(8,128)}, u32[]{:S(2)}) copy-start(f32[12,512]{1,0:T(8,128)} %refs_4_.1) | copy-start | bytes 73732
  17.5 65.9 %copy-start.6 = (f32[12,512]{1,0:T(8,128)S(1)}, f32[12,512]{1,0:T(8,128)}, u32[]{:S(2)}) copy-start(f32[12,512]{1,0:T(8,128)} %refs_5_.1) | copy-start | bytes 73732
  17.5 65.9 %copy-start.7 = (f32[16,192]{1,0:T(8,128)S(1)}, f32[16,192]{1,0:T(8,128)}, u32[]{:S(2)}) copy-start(f32[16,192]{1,0:T(8,128)} %refs_7_.1) | copy-start | bytes 36868
  17.5 65.9 %copy-start.8 = (f32[16,192]{1,0:T(8,128)S(1)}, f32[16,192]{1,0:T(8,128)}, u32[]{:S(2)}) copy-start(f32[16,192]{1,0:T(8,128)} %refs_8_.1) | copy-start | bytes 36868
  17.5 65.8 %copy-start.9 = (f32[128]{0:T(128)S(1)}, f32[128]{0:T(128)}, u32[]{:S(2)}) copy-start(f32[128]{0:T(128)} %param.21) | copy-start | bytes 1540
  17.5 65.8 %copy-start.10 = (f32[128]{0:T(128)S(1)}, f32[128]{0:T(128)}, u32[]{:S(2)}) copy-start(f32[128]{0:T(128)} %param.28) | copy-start | bytes 1540
  17.6 65.8 %copy-start.11 = (f32[128]{0:T(128)S(1)}, f32[128]{0:T(128)}, u32[]{:S(2)}) copy-start(f32[128]{0:T(128)} %param.29) | copy-start | bytes 1540

commit v6 on v5

--- a/solution.py
+++ b/solution.py
@@ -25,16 +25,36 @@
 
 def layer_kernel(
     group,
-    x_ref, mask_ref, g_ref, full_ref,
-    y_ref, dx_ref, packed_ref,
+    x_hbm, mask_hbm, g_hbm, full_hbm,
+    y_hbm, dx_hbm, packed_ref,
     big, w2f, vec_s, wqkv_ref, wo_ref, w1_ref, w2_ref,
     wqkvt, wot, w1t, w2t, cols, n1a, n2a, oa, ha, e_s,
     gqkv_ref, go_ref, g1_ref, g2_ref, ln_acc, pack_s, gqkvt_ref, g1t_ref,
     q_s, k_s, v_s, d_s, c_s, dqkv_s, o_s, inv_s, et_s,
+    full_ref, mask_ref, x_b, g_b, y_b, dx_b, once_sem, in_sem, out_sem,
 ):
     step = pl.program_id(0)
-    length = x_ref.shape[2]
-    width = x_ref.shape[1]
+    length = x_hbm.shape[2]
+    width = x_hbm.shape[1]
+    slot = lax.rem(step, 2)
+    steps = x_hbm.shape[0] // group
+    x_ref, g_ref, y_ref, dx_ref = (b.at[slot] for b in (x_b, g_b, y_b, dx_b))
+
+    def arriving(index):
+        into = lax.rem(index, 2)
+        rows = pl.ds(index * group, group)
+        return [
+            pltpu.make_async_copy(x_hbm.at[rows], x_b.at[into], in_sem.at[0, into]),
+            pltpu.make_async_copy(g_hbm.at[rows], g_b.at[into], in_sem.at[1, into]),
+        ]
+
+    def leaving(index):
+        out_of = lax.rem(index, 2)
+        rows = pl.ds(index * group, group)
+        return [
+            pltpu.make_async_copy(y_b.at[out_of], y_hbm.at[rows], out_sem.at[0, out_of]),
+            pltpu.make_async_copy(dx_b.at[out_of], dx_hbm.at[rows], out_sem.at[1, out_of]),
+        ]
     head = width // H
     tokens = group * LANES
     factor = float(head) ** (-0.5)
@@ -42,6 +62,14 @@
 
     @pl.when(step == 0)
     def _():
+        first = [
+            pltpu.make_async_copy(full_hbm, full_ref, once_sem.at[0]),
+            pltpu.make_async_copy(mask_hbm, mask_ref, once_sem.at[1]),
+        ]
+        for copy in first + arriving(0):
+            copy.start()
+        for copy in first:
+            copy.wait()
         shards, _, block_rows, _ = full_ref.shape
         depth = width // shards
         extra = block_rows - depth
@@ -84,6 +112,19 @@
         g1t_ref[...] = jnp.zeros_like(g1t_ref)
         g2_ref[...] = jnp.zeros_like(g2_ref)
         ln_acc[...] = jnp.zeros_like(ln_acc)
+
+    @pl.when(step + 1 < pl.num_programs(0))
+    def _():
+        for copy in arriving(step + 1):
+            copy.start()
+
+    for copy in arriving(step):
+        copy.wait()
+
+    @pl.when(step > 1)
+    def _():
+        for copy in leaving(step - 2):
+            copy.wait()
 
     def wide(ref, g):
         t = ref[g]
@@ -251,6 +292,9 @@
     for g in range(group):
         dx_ref[g] = dx[:, g * LANES : g * LANES + length]
 
+    for copy in leaving(step):
+        copy.start()
+
     @pl.when(step == pl.num_programs(0) - 1)
     def _():
         gqkv_ref[...] = gqkvt_ref[...].T
@@ -282,18 +326,21 @@
             pack_s[w, depth : depth + 1, 4 * width : 4 * width + per_vec] = vec[:, w * per_vec : (w + 1) * per_vec]
         for j in range(2):
             packed_ref[:, j] = pack_s[:, :, j * half : (j + 1) * half].astype(BF16)
+        for copy in leaving(step) + (leaving(step - 1) if steps > 1 else []):
+            copy.wait()
 
 
 def run_layer(x, mask, dout, full, group):
     samples, width, length = x.shape
     tokens = group * LANES
     whole = lambda a: pl.BlockSpec(a.shape, lambda i: (0,) * a.ndim)
-    per = pl.BlockSpec((group, width, length), lambda i: (i, 0, 0))
+    apart = pl.BlockSpec(memory_space=pl.ANY)
+    block = (group, width, length)
     return pl.pallas_call(
         functools.partial(layer_kernel, group),
         grid=(samples // group,),
-        in_specs=[per, whole(mask), per, whole(full)],
-        out_specs=[per, per, whole(full)],
+        in_specs=[apart] * 4,
+        out_specs=[apart, apart, whole(full)],
         out_shape=[jax.ShapeDtypeStruct(x.shape, BF16)] * 2 + [jax.ShapeDtypeStruct(full.shape, BF16)],
         scratch_shapes=[
             pltpu.VMEM((width, 4 * width + 2 * FH), F32),
@@ -330,6 +377,15 @@
             pltpu.VMEM((width, tokens), F32),
             pltpu.VMEM((group, H // 2, 2 * LANES), F32),
             pltpu.VMEM((group, H // 2, LANES, 2 * LANES), BF16),
+            pltpu.VMEM(full.shape, BF16),
+            pltpu.VMEM(mask.shape, jnp.int32),
+            pltpu.VMEM((2,) + block, BF16),
+            pltpu.VMEM((2,) + block, BF16),
+            pltpu.VMEM((2,) + block, BF16),
+            pltpu.VMEM((2,) + block, BF16),
+            pltpu.SemaphoreType.DMA((2,)),
+            pltpu.SemaphoreType.DMA((2, 2)),
+            pltpu.SemaphoreType.DMA((2, 2)),
         ],
         compiler_params=pltpu.CompilerParams(vmem_limit_bytes=60 * 1024 * 1024),
         name="layer",
@@ -452,16 +508,16 @@
     for k in range(1, chips):
         third[k].wait_recv()
         total = total + wide_buf[k].astype(F32)
-    narrow_buf[mine] = total
+    narrow_buf[mine] = total.astype(BF16)
     slot = narrow_buf.at[mine]
     fourth = [send(slot, slot, send3.at[j], recv3.at[j], other) for j, other in enumerate(others)]
     for copy in fourth:
         copy.wait_recv()
     lanes = total.shape[1]
     for h in range(2):
-        result = narrow_buf[h]
+        result = narrow_buf[h].astype(F32)
         for j in range(h + 2, copies_of, 2):
-            result = result + narrow_buf[j]
+            result = result + narrow_buf[j].astype(F32)
         out_ref[:, h * lanes : (h + 1) * lanes] = result
     for copy in list(first.values()) + list(second.values()) + list(third.values()) + fourth:
         copy.wait_send()
@@ -479,7 +535,7 @@
         in_specs=[pl.BlockSpec(memory_space=pl.ANY)],
         out_specs=pl.BlockSpec(memory_space=pltpu.VMEM),
         scratch_shapes=[pltpu.VMEM(packed.shape, BF16), pltpu.VMEM((chips, 2, rows, lanes), BF16), part(F32),
-                        part(BF16), part(BF16), part(BF16), part(BF16), pltpu.VMEM((copies_of, rows, lanes), F32),
+                        part(BF16), part(BF16), part(BF16), part(BF16), pltpu.VMEM((copies_of, rows, lanes), BF16),
                         pltpu.SemaphoreType.DMA] + [sems] * 6 + [few] * 2,
         compiler_params=pltpu.CompilerParams(collective_id=1, has_side_effects=True, vmem_limit_bytes=56000000),
         name="reduce",

time: 84.6 us -> 83.6 us (0.988)
  Pallas kernels: 83.5 us -> 82.4 us
where the time goes in v6:
time: 83.6 us; the launch traced here: 83.4 us
  Pallas kernels  82.4 us (99%)
  between operations  0.86 us (1%)
    pallas_call x1, Pallas kernels, run_layer(): pl.pallas_call(functools.partial(layer_kernel, group), grid=(samples // g...  49.3 us
    pallas_call x1, Pallas kernels, gather(): pl.pallas_call(functools.partial(gather_kernel, n, copies_of), out_shape=...  16.8 us
    pallas_call x1, Pallas kernels, reduce_shares(): pl.pallas_call(functools.partial(reduce_kernel, n, copies_of), out_shape=...  15.4 us

profile of v6, /device:TPU:0, one launch (start us, length us, event | category | flops | bytes accessed | tf_op | source)
XLA Modules:
  0.0 83.4 jit_solution(16178157958711781578)
XLA Ops:
  0.6 16.8 %gather.1.full_hbm = bf16[16,2,16,640]{3,2,1,0:T(8,128)(2,1)} custom-call(f32[12,4,192]{2,1,0:T(4,128)} %bitcast.16, f32[12,512]{1,0:T(8,128)} %refs_3_.1, f32[16,192]{1,0:T(8,128)} %refs_6_.1, f32[1,128]{1,0:T(1,128)} %bitcast.20), custom_call_target="tpu_custom_call" | custom-call | tf_op jit(solution)/shard_map/gather/pallas_call | solution.py:471
  17.4 0.0 copy-start
  17.4 0.0 copy-start.1
  17.4 0.0 copy-start.2
  17.5 0.0 copy-start.3
  17.5 0.0 copy-start.4
  17.5 0.0 copy-start.5
  17.5 0.0 copy-start.6
  17.5 0.0 copy-start.7
  17.5 0.0 copy-start.8
  17.5 0.0 copy-start.9
  17.5 0.0 copy-start.10
  17.6 0.0 copy-start.11
  17.6 49.3 %layer.1 = (bf16[64,192,119]{2,1,0:T(8,128)(2,1)}, bf16[64,192,119]{2,1,0:T(8,128)(2,1)}, bf16[16,2,16,640]{3,2,1,0:T(8,128)(2,1)}) custom-call(bf16[64,192,119]{2,1,0:T(8,128)(2,1)} %bitcast.24, s32[64,119]{1,0:T(8,128)} %mask_hbm.1, bf16[64,192,119]{2,1,0:T(8,128)(2,1)} %bitcast.25, bf16[16,2,16,640]{3,2,1,0:T(8,128)(2,1)} %gather.1.full_hbm), custom_call_target="tpu_custom_call" | custom-call | tf_op jit(solution)/shard_map/layer/pallas_call | solution.py:339
  66.8 15.4 %reduce.1.grad_ref = f32[16,1280]{1,0:T(8,128)S(1)} custom-call(bf16[16,2,16,640]{3,2,1,0:T(8,128)(2,1)} %get-tuple-element.31.part_hbm), custom_call_target="tpu_custom_call" | custom-call | tf_op jit(solution)/shard_map/reduce/pallas_call | solution.py:532
  82.2 0.0 copy-done
  82.3 0.0 copy-done.1
  82.3 0.0 copy-done.2
  82.3 0.0 copy-done.3
  82.3 0.0 copy-done.4
  82.3 0.0 copy-done.5
  82.3 0.0 copy-done.6
  82.3 0.0 copy-done.7
  82.4 1.0 %update.1 = (f32[12,4,192]{2,1,0:T(4,128)}, f32[12,4,192]{2,1,0:T(4,128)}, f32[12,4,192]{2,1,0:T(4,128)}, f32[12,512]{1,0:T(8,128)}, f32[12,512]{1,0:T(8,128)}, ...) custom-call(f32[16,1280]{1,0:T(8,128)S(1)} %reduce.1.grad_ref, ...), custom_call_target="tpu_custom_call" | custom-call | tf_op jit(solution)/shard_map/update/pallas_call | solution.py:573
  (4 shorter events, 0.0 us)
Async XLA Ops:
  17.4 64.8 %copy-start = (f32[4,12,192]{2,0,1:T(4,128)S(1)}, f32[4,12,192]{2,0,1:T(4,128)}, u32[]{:S(2)}) copy-start(f32[4,12,192]{2,0,1:T(4,128)} %param.18) | copy-start | bytes 110596
  17.4 64.8 %copy-start.1 = (f32[12,512]{1,0:T(8,128)S(1)}, f32[12,512]{1,0:T(8,128)}, u32[]{:S(2)}) copy-start(f32[12,512]{1,0:T(8,128)} %refs_3_.1) | copy-start | bytes 73732
  17.4 64.8 %copy-start.2 = (f32[16,192]{1,0:T(8,128)S(1)}, f32[16,192]{1,0:T(8,128)}, u32[]{:S(2)}) copy-start(f32[16,192]{1,0:T(8,128)} %refs_6_.1) | copy-start | bytes 36868
  17.5 64.8 %copy-start.3 = (f32[4,12,192]{2,0,1:T(4,128)S(1)}, f32[4,12,192]{2,0,1:T(4,128)}, u32[]{:S(2)}) copy-start(f32[4,12,192]{2,0,1:T(4,128)} %param.22) | copy-start | bytes 110596
  17.5 64.8 %copy-start.4 = (f32[4,12,192]{2,0,1:T(4,128)S(1)}, f32[4,12,192]{2,0,1:T(4,128)}, u32[]{:S(2)}) copy-start(f32[4,12,192]{2,0,1:T(4,128)} %param.23) | copy-start | bytes 110596
  17.5 64.8 %copy-start.5 = (f32[12,512]{1,0:T(8,128)S(1)}, f32[12,512]{1,0:T(8,128)}, u32[]{:S(2)}) copy-start(f32[12,512]{1,0:T(8,128)} %refs_4_.1) | copy-start | bytes 73732
  17.5 64.8 %copy-start.6 = (f32[12,512]{1,0:T(8,128)S(1)}, f32[12,512]{1,0:T(8,128)}, u32[]{:S(2)}) copy-start(f32[12,512]{1,0:T(8,128)} %refs_5_.1) | copy-start | bytes 73732
  17.5 64.8 %copy-start.7 = (f32[16,192]{1,0:T(8,128)S(1)}, f32[16,192]{1,0:T(8,128)}, u32[]{:S(2)}) copy-start(f32[16,192]{1,0:T(8,128)} %refs_7_.1) | copy-start | bytes 36868
  17.5 64.8 %copy-start.8 = (f32[16,192]{1,0:T(8,128)S(1)}, f32[16,192]{1,0:T(8,128)}, u32[]{:S(2)}) copy-start(f32[16,192]{1,0:T(8,128)} %refs_8_.1) | copy-start | bytes 36868
  17.5 64.8 %copy-start.9 = (f32[128]{0:T(128)S(1)}, f32[128]{0:T(128)}, u32[]{:S(2)}) copy-start(f32[128]{0:T(128)} %param.21) | copy-start | bytes 1540
  17.5 64.8 %copy-start.10 = (f32[128]{0:T(128)S(1)}, f32[128]{0:T(128)}, u32[]{:S(2)}) copy-start(f32[128]{0:T(128)} %param.28) | copy-start | bytes 1540
  17.6 64.8 %copy-start.11 = (f32[128]{0:T(128)S(1)}, f32[128]{0:T(128)}, u32[]{:S(2)}) copy-start(f32[128]{0:T(128)} %param.29) | copy-start | bytes 1540

commit v7 on v6

--- a/solution.py
+++ b/solution.py
@@ -11,7 +11,7 @@
 STEP = 10
 LANES = 128
 FORWARD = (0, 1, 7, 8, 9, 12)
-BACKWARD = (0, 1, 1, 5, 6, 9)
+BACKWARD = (0, 0, 1, 4, 5, 8)
 GROUP = 16
 F32 = jnp.float32
 BF16 = jnp.bfloat16
@@ -112,6 +112,7 @@
         g1t_ref[...] = jnp.zeros_like(g1t_ref)
         g2_ref[...] = jnp.zeros_like(g2_ref)
         ln_acc[...] = jnp.zeros_like(ln_acc)
+        pack_s[...] = jnp.zeros_like(pack_s)
 
     @pl.when(step + 1 < pl.num_programs(0))
     def _():
@@ -314,7 +315,6 @@
         depth = width // shards
         extra = block_rows - depth
         per_vec = vec.shape[1] // shards
-        pack_s[...] = jnp.zeros_like(pack_s)
         for w in range(shards):
             r = slice(w * depth, (w + 1) * depth)
             pack_s[w, :depth, : 4 * width] = jnp.concatenate([gqkv_ref[r, :], go_ref[r, :]], axis=1)
@@ -442,19 +442,25 @@
     out_ref[me, 0] = block[:, :lanes]
     out_ref[me, 1] = block[:, lanes:]
     pl.semaphore_wait(pltpu.get_barrier_semaphore(), len(met))
-    own = out_ref.at[me, half]
+    whole, own = out_ref.at[me], out_ref.at[me, half]
+    far, near = range(chips // 2, chips), range(1, chips // 2)
     copies = {}
-    for k in reversed(range(1, chips)):
+    for k in far:
         copies[k] = send(own, own, send1.at[k], recv1.at[k], {"wide": peer(k)})
-    whole = out_ref.at[me]
+    for k in near:
+        copies[k] = send(whole, whole, send1.at[k], recv1.at[k], {"wide": peer(k)})
     passed = [send(whole, whole, send2.at[0], recv2.at[0], sibling)]
     crossed = {}
-    for k in range(1, chips):
+    for k in near:
+        copies[k].wait_recv()
+        got = out_ref.at[peer(k)]
+        passed.append(send(got, got, send2.at[k], recv2.at[k], sibling))
+    for k in far:
         copies[k].wait_recv()
         got = out_ref.at[peer(k), half]
         crossed[k] = send(got, got, send3.at[k], recv3.at[k], twin)
         passed.append(send(got, got, send2.at[k], recv2.at[k], sibling))
-    for k in range(1, chips):
+    for k in far:
         crossed[k].wait_recv()
         got = out_ref.at[peer(k), 1 - half]
         passed.append(send(got, got, send4.at[k], recv4.at[k], sibling))
@@ -481,7 +487,8 @@
 
 
 def reduce_kernel(n, copies_of, part_hbm, out_ref, part_ref, core_buf, keep_buf, turn_buf, twin_buf, sum_buf,
-                  wide_buf, narrow_buf, load, send0, recv0, send1, recv1, send2, recv2, send3, recv3):
+                  far_buf, near_out, near_buf, late_out, late_buf, narrow_buf, load,
+                  send0, recv0, send1, recv1, send2, recv2, send3, recv3, send4, recv4, late_sem):
     me, mine, core, chips, peer, half, sibling, twin = places(n, copies_of)
     others = [{"narrow": lax.rem(mine + j, copies_of)} for j in range(1, copies_of)]
     met = [{"wide": peer(k)} for k in range(1, chips)] + [sibling] + others
@@ -490,27 +497,45 @@
     mine_parts.start()
     mine_parts.wait()
     pl.semaphore_wait(pltpu.get_barrier_semaphore(), len(met))
-    order = list(reversed(range(chips)))
-    first, second, third = {}, {}, {}
-    for k in order:
+    far = list(reversed(range(chips // 2, chips)))
+    near = list(reversed(range(1, chips // 2)))
+    first, second, third, direct = {}, {}, {}, {}
+    for k in far + near + [0]:
         first[k] = send(part_ref.at[peer(k) + 1 - 2 * core], core_buf.at[k], send0.at[k], recv0.at[k], sibling)
-    for k in order:
+
+    def chip_sum(k, h):
+        return part_ref[peer(k), h].astype(F32) + core_buf[k, h].astype(F32)
+
+    for k in far:
         first[k].wait_recv()
-        turn_buf[k] = (part_ref[peer(k), 1 - half].astype(F32) + core_buf[k, 1 - half].astype(F32)).astype(BF16)
+        turn_buf[k] = chip_sum(k, 1 - half).astype(BF16)
         second[k] = send(turn_buf.at[k], twin_buf.at[k], send1.at[k], recv1.at[k], twin)
-        keep_buf[k] = part_ref[peer(k), half].astype(F32) + core_buf[k, half].astype(F32)
-    for k in order:
+        keep_buf[k] = chip_sum(k, half)
+    for k in near:
+        first[k].wait_recv()
+        for h in range(2):
+            near_out[k, h] = chip_sum(k, h).astype(BF16)
+        direct[k] = send(near_out.at[k], near_buf.at[k], send2.at[k], recv2.at[k], {"wide": peer(k)})
+    first[0].wait_recv()
+    for k in far:
         second[k].wait_recv()
-        total = keep_buf[k] + twin_buf[k].astype(F32)
-        if k:
-            sum_buf[k] = total.astype(BF16)
-            third[k] = send(sum_buf.at[k], wide_buf.at[k], send2.at[k], recv2.at[k], {"wide": peer(k)})
-    for k in range(1, chips):
+        sum_buf[k] = (keep_buf[k] + twin_buf[k].astype(F32)).astype(BF16)
+        third[k] = send(sum_buf.at[k], far_buf.at[k], send3.at[k], recv3.at[k], {"wide": peer(k)})
+    total, across = chip_sum(0, half), chip_sum(0, 1 - half)
+    for k in near:
+        direct[k].wait_recv()
+        total = total + near_buf[k, half].astype(F32)
+        across = across + near_buf[k, 1 - half].astype(F32)
+    late_out[...] = across.astype(BF16)
+    late = send(late_out, late_buf, late_sem.at[0], late_sem.at[1], twin)
+    for k in far:
         third[k].wait_recv()
-        total = total + wide_buf[k].astype(F32)
+        total = total + far_buf[k].astype(F32)
+    late.wait_recv()
+    total = total + late_buf[...].astype(F32)
     narrow_buf[mine] = total.astype(BF16)
     slot = narrow_buf.at[mine]
-    fourth = [send(slot, slot, send3.at[j], recv3.at[j], other) for j, other in enumerate(others)]
+    fourth = [send(slot, slot, send4.at[j], recv4.at[j], other) for j, other in enumerate(others)]
     for copy in fourth:
         copy.wait_recv()
     lanes = total.shape[1]
@@ -519,7 +544,10 @@
         for j in range(h + 2, copies_of, 2):
             result = result + narrow_buf[j].astype(F32)
         out_ref[:, h * lanes : (h + 1) * lanes] = result
-    for copy in list(first.values()) + list(second.values()) + list(third.values()) + fourth:
+    for group_of in (first, second, third, direct):
+        for copy in group_of.values():
+            copy.wait_send()
+    for copy in [late] + fourth:
         copy.wait_send()
 
 
@@ -529,14 +557,16 @@
     sems = pltpu.SemaphoreType.DMA((chips,))
     few = pltpu.SemaphoreType.DMA((copies_of,))
     part = lambda kind: pltpu.VMEM((chips, rows, lanes), kind)
+    pair = pltpu.VMEM((chips, 2, rows, lanes), BF16)
+    one = pltpu.VMEM((rows, lanes), BF16)
     return pl.pallas_call(
         functools.partial(reduce_kernel, n, copies_of),
         out_shape=jax.ShapeDtypeStruct((rows, 2 * lanes), F32),
         in_specs=[pl.BlockSpec(memory_space=pl.ANY)],
         out_specs=pl.BlockSpec(memory_space=pltpu.VMEM),
-        scratch_shapes=[pltpu.VMEM(packed.shape, BF16), pltpu.VMEM((chips, 2, rows, lanes), BF16), part(F32),
-                        part(BF16), part(BF16), part(BF16), part(BF16), pltpu.VMEM((copies_of, rows, lanes), BF16),
-                        pltpu.SemaphoreType.DMA] + [sems] * 6 + [few] * 2,
+        scratch_shapes=[pltpu.VMEM(packed.shape, BF16), pair, part(F32), part(BF16), part(BF16), part(BF16),
+                        part(BF16), pair, pair, one, one, pltpu.VMEM((copies_of, rows, lanes), BF16),
+                        pltpu.SemaphoreType.DMA] + [sems] * 8 + [few] * 2 + [pltpu.SemaphoreType.DMA((2,))],
         compiler_params=pltpu.CompilerParams(collective_id=1, has_side_effects=True, vmem_limit_bytes=56000000),
         name="reduce",
     )(packed)

time: 83.6 us -> 83.8 us (level)
  no operation moved by 1% of the time
where the time goes in v7:
time: 83.8 us; the launch traced here: 83.5 us
  Pallas kernels  82.6 us (99%)
  between operations  0.86 us (1%)
    pallas_call x1, Pallas kernels, run_layer(): pl.pallas_call(functools.partial(layer_kernel, group), grid=(samples // g...  49.3 us
    pallas_call x1, Pallas kernels, gather(): pl.pallas_call(functools.partial(gather_kernel, n, copies_of), out_shape=...  16.7 us
    pallas_call x1, Pallas kernels, reduce_shares(): pl.pallas_call(functools.partial(reduce_kernel, n, copies_of), out_shape=...  15.6 us

profile of v7, /device:TPU:0, one launch (start us, length us, event | category | flops | bytes accessed | tf_op | source)
XLA Modules:
  0.0 83.5 jit_solution(568165649520765747)
XLA Ops:
  0.6 16.7 %gather.1.full_hbm = bf16[16,2,16,640]{3,2,1,0:T(8,128)(2,1)} custom-call(f32[12,4,192]{2,1,0:T(4,128)} %bitcast.16, f32[12,512]{1,0:T(8,128)} %refs_3_.1, f32[16,192]{1,0:T(8,128)} %refs_6_.1, f32[1,128]{1,0:T(1,128)} %bitcast.20), custom_call_target="tpu_custom_call" | custom-call | tf_op jit(solution)/shard_map/gather/pallas_call | solution.py:477
  17.4 0.0 copy-start
  17.4 0.0 copy-start.1
  17.4 0.0 copy-start.2
  17.4 0.0 copy-start.3
  17.4 0.0 copy-start.4
  17.5 0.0 copy-start.5
  17.5 0.0 copy-start.6
  17.5 0.0 copy-start.7
  17.5 0.0 copy-start.8
  17.5 0.0 copy-start.9
  17.5 0.0 copy-start.10
  17.5 0.0 copy-start.11
  17.5 49.3 %layer.1 = (bf16[64,192,119]{2,1,0:T(8,128)(2,1)}, bf16[64,192,119]{2,1,0:T(8,128)(2,1)}, bf16[16,2,16,640]{3,2,1,0:T(8,128)(2,1)}) custom-call(bf16[64,192,119]{2,1,0:T(8,128)(2,1)} %bitcast.24, s32[64,119]{1,0:T(8,128)} %mask_hbm.1, bf16[64,192,119]{2,1,0:T(8,128)(2,1)} %bitcast.25, bf16[16,2,16,640]{3,2,1,0:T(8,128)(2,1)} %gather.1.full_hbm), custom_call_target="tpu_custom_call" | custom-call | tf_op jit(solution)/shard_map/layer/pallas_call | solution.py:339
  66.8 15.6 %reduce.1.grad_ref = f32[16,1280]{1,0:T(8,128)S(1)} custom-call(bf16[16,2,16,640]{3,2,1,0:T(8,128)(2,1)} %get-tuple-element.31.part_hbm), custom_call_target="tpu_custom_call" | custom-call | tf_op jit(solution)/shard_map/reduce/pallas_call | solution.py:562
  82.4 0.0 copy-done
  82.4 0.0 copy-done.1
  82.4 0.0 copy-done.2
  82.5 0.0 copy-done.3
  82.5 0.0 copy-done.4
  82.5 0.0 copy-done.5
  82.5 0.0 copy-done.6
  82.5 0.0 copy-done.7
  82.5 1.0 %update.1 = (f32[12,4,192]{2,1,0:T(4,128)}, f32[12,4,192]{2,1,0:T(4,128)}, f32[12,4,192]{2,1,0:T(4,128)}, f32[12,512]{1,0:T(8,128)}, f32[12,512]{1,0:T(8,128)}, ...) custom-call(f32[16,1280]{1,0:T(8,128)S(1)} %reduce.1.grad_ref, ...), custom_call_target="tpu_custom_call" | custom-call | tf_op jit(solution)/shard_map/update/pallas_call | solution.py:603
  (4 shorter events, 0.0 us)
Async XLA Ops:
  17.4 65.0 %copy-start = (f32[4,12,192]{2,0,1:T(4,128)S(1)}, f32[4,12,192]{2,0,1:T(4,128)}, u32[]{:S(2)}) copy-start(f32[4,12,192]{2,0,1:T(4,128)} %param.18) | copy-start | bytes 110596
  17.4 65.0 %copy-start.1 = (f32[12,512]{1,0:T(8,128)S(1)}, f32[12,512]{1,0:T(8,128)}, u32[]{:S(2)}) copy-start(f32[12,512]{1,0:T(8,128)} %refs_3_.1) | copy-start | bytes 73732
  17.4 65.0 %copy-start.2 = (f32[16,192]{1,0:T(8,128)S(1)}, f32[16,192]{1,0:T(8,128)}, u32[]{:S(2)}) copy-start(f32[16,192]{1,0:T(8,128)} %refs_6_.1) | copy-start | bytes 36868
  17.4 65.0 %copy-start.3 = (f32[4,12,192]{2,0,1:T(4,128)S(1)}, f32[4,12,192]{2,0,1:T(4,128)}, u32[]{:S(2)}) copy-start(f32[4,12,192]{2,0,1:T(4,128)} %param.22) | copy-start | bytes 110596
  17.4 65.0 %copy-start.4 = (f32[4,12,192]{2,0,1:T(4,128)S(1)}, f32[4,12,192]{2,0,1:T(4,128)}, u32[]{:S(2)}) copy-start(f32[4,12,192]{2,0,1:T(4,128)} %param.23) | copy-start | bytes 110596
  17.5 65.0 %copy-start.5 = (f32[12,512]{1,0:T(8,128)S(1)}, f32[12,512]{1,0:T(8,128)}, u32[]{:S(2)}) copy-start(f32[12,512]{1,0:T(8,128)} %refs_4_.1) | copy-start | bytes 73732
  17.5 65.0 %copy-start.6 = (f32[12,512]{1,0:T(8,128)S(1)}, f32[12,512]{1,0:T(8,128)}, u32[]{:S(2)}) copy-start(f32[12,512]{1,0:T(8,128)} %refs_5_.1) | copy-start | bytes 73732
  17.5 65.0 %copy-start.7 = (f32[16,192]{1,0:T(8,128)S(1)}, f32[16,192]{1,0:T(8,128)}, u32[]{:S(2)}) copy-start(f32[16,192]{1,0:T(8,128)} %refs_7_.1) | copy-start | bytes 36868
  17.5 65.0 %copy-start.8 = (f32[16,192]{1,0:T(8,128)S(1)}, f32[16,192]{1,0:T(8,128)}, u32[]{:S(2)}) copy-start(f32[16,192]{1,0:T(8,128)} %refs_8_.1) | copy-start | bytes 36868
  17.5 65.0 %copy-start.9 = (f32[128]{0:T(128)S(1)}, f32[128]{0:T(128)}, u32[]{:S(2)}) copy-start(f32[128]{0:T(128)} %param.21) | copy-start | bytes 1540
  17.5 65.0 %copy-start.10 = (f32[128]{0:T(128)S(1)}, f32[128]{0:T(128)}, u32[]{:S(2)}) copy-start(f32[128]{0:T(128)} %param.28) | copy-start | bytes 1540
  17.5 65.0 %copy-start.11 = (f32[128]{0:T(128)S(1)}, f32[128]{0:T(128)}, u32[]{:S(2)}) copy-start(f32[128]{0:T(128)} %param.29) | copy-start | bytes 1540
